TPU v7x, 32 devices: a whole 2x2x4 slice. The times are simulated.
32 devices in a mesh: head: 2 (over x), seq: 16 (over z, y, core).
Axes of the slice: x: 2, y: 2, z: 4, core: 2. Of those that a mesh axis runs over, the one named last changes fastest.
Arguments:
- activations: bfloat16 [2048, 4096], P('seq'), may hold values from -6 to 6
- w_query: bfloat16 [3, 4096, 2048], P(None, 'seq', 'head'), may hold values from -32 to 32
- w_keyval: bfloat16 [3, 4096, 1024], P(None, 'seq'), may hold values from -32 to 32
- q_gain: float32 [3, 2048], P(None, 'head'), may hold values from 0.1 to 1.9
- k_gain: float32 [3, 512], replicated, may hold values from 0.1 to 1.9
- stream_ids: int32 [2048], P('seq'), may hold values from 0 to 2
- local_times: int32 [2048], P('seq'), may hold values from 0 to 31
- block_map: int32 [32], replicated, may hold values from 0 to 31, each once
Outputs:
- attended: bfloat16 [2048, 2048], P('seq', 'head')
Inputs may be any that keep to these rules, and one draw needn't show every extreme that they name: `block_map`: a permutation of the block indices.
All inputs are finite; a program needn't handle non-finite values.
Results may differ from a plain program's by a relative error of at most 0.012.
The roundings to bfloat16 on the way count: a program that leaves them out, or rounds other values in their place, can miss the bound.
Values may be sent and summed in bfloat16 or wider, within the bound.
No kernel may reach another device: no remote copies, remote signals or barrier semaphores. Data moves between devices by JAX's collectives and lax.ppermute only.
A program may use at most 128 MiB of HBM per device.

v0:
```python
import math

import jax
import jax.numpy as jnp
from jax import lax
from jax.sharding import PartitionSpec as P

HEADS = 16
KV_HEADS = 4
HEAD_DIM = 128
STREAMS = 3
FRAMES = 32


epsilon = 1e-06


def body(activations, w_query, w_keyval, q_gain, k_gain, stream_ids, local_times, block_map):
    row_count = activations.shape[0]
    block_rows = row_count // 2
    group_size = HEADS // KV_HEADS
    q_local = w_query.shape[2] // HEAD_DIM
    per_group = min(group_size, q_local)
    kv_local = q_local // per_group
    replicas = max(1, lax.axis_size("head") // KV_HEADS)
    head_index = lax.axis_index("head")
    first_group = head_index * q_local // group_size
    kv_weights = lax.dynamic_slice_in_dim(
        w_keyval, first_group * (2 * HEAD_DIM), kv_local * 2 * HEAD_DIM, 2
    )
    kv_gain = lax.dynamic_slice_in_dim(k_gain, first_group * HEAD_DIM, kv_local * HEAD_DIM, 1)
    position = lax.axis_index("seq")
    slot_ids = position * 2 + jnp.arange(row_count, dtype=jnp.int32) // block_rows
    slot_match = slot_ids[:, None] == jnp.arange(block_map.shape[0], dtype=jnp.int32)[None, :]
    query_times = (
        jnp.sum(jnp.where(slot_match, block_map[None, :], 0), axis=1) * FRAMES + local_times
    )
    stream_match = stream_ids[:, None] == jnp.arange(STREAMS, dtype=jnp.int32)[None, :]
    spread = activations[:, None, :] * stream_match.astype(jnp.bfloat16)[:, :, None]
    query_sum = jnp.einsum(
        "rsd,sdc->rc",
        spread,
        lax.all_gather(w_query, "seq", axis=1, tiled=True),
        preferred_element_type=jnp.float32,
    )
    pair_sum = jnp.einsum(
        "rsd,sdc->rc",
        spread,
        lax.all_gather(kv_weights, "seq", axis=1, tiled=True),
        preferred_element_type=jnp.float32,
    )
    key_value = pair_sum
    key_value = key_value.reshape(row_count, kv_local, 2, HEAD_DIM)
    keys_raw = key_value[:, :, 0].reshape(row_count, kv_local * HEAD_DIM)
    values = key_value[:, :, 1].astype(jnp.bfloat16)
    key_part = jnp.where(
        head_index % replicas == 0, jnp.sum(keys_raw * keys_raw, axis=1), jnp.float32(0.0)
    )
    query_sq, key_sq = lax.psum((jnp.sum(query_sum * query_sum, axis=1), key_part), "head")
    onehot = stream_match.astype(jnp.float32)
    q_scale = jnp.dot(onehot, q_gain, precision=lax.Precision.HIGHEST)
    k_scale = jnp.dot(onehot, kv_gain, precision=lax.Precision.HIGHEST)
    q_normed = (
        query_sum * lax.rsqrt(query_sq / (HEADS * HEAD_DIM) + epsilon)[:, None] * q_scale
    ).astype(jnp.bfloat16)
    q_normed = q_normed.reshape(row_count, kv_local, per_group, HEAD_DIM)
    k_normed = (
        keys_raw * lax.rsqrt(key_sq / (KV_HEADS * HEAD_DIM) + epsilon)[:, None] * k_scale
    ).astype(jnp.bfloat16)
    k_normed = k_normed.reshape(row_count, kv_local, HEAD_DIM)
    score_scale = 1.0 / math.sqrt(HEAD_DIM)
    run_max = jnp.full((row_count, kv_local, per_group), -1e30, jnp.float32)
    key_part_now = lax.all_gather(k_normed, "seq", axis=0, tiled=True)
    value_part = lax.all_gather(values, "seq", axis=0, tiled=True)
    key_times = lax.all_gather(query_times, "seq", axis=0, tiled=True)
    scores = (
        jnp.einsum("rkgd,nkd->rkgn", q_normed, key_part_now, preferred_element_type=jnp.float32)
        * score_scale
    )
    visible = key_times[None, None, None, :] <= query_times[:, None, None, None]
    new_max = jnp.maximum(run_max, jnp.max(jnp.where(visible, scores, -1e30), axis=3))
    exp_terms = jnp.where(visible, jnp.exp(scores - new_max[..., None]), jnp.float32(0.0))
    run_sum = jnp.sum(exp_terms, axis=3)
    weighted = jnp.einsum(
        "rkgn,nkd->rkgd",
        exp_terms.astype(jnp.bfloat16),
        value_part,
        preferred_element_type=jnp.float32,
    )
    run_max, run_sum, weighted = (new_max, run_sum, weighted)
    return (
        (weighted / run_sum[..., None])
        .reshape(row_count, kv_local * per_group * HEAD_DIM)
        .astype(jnp.bfloat16)
    )


def solution(mesh):
    placed = (
        P("seq", None),
        P(None, "seq", "head"),
        P(None, "seq", None),
        P(None, "head"),
        P(),
        P("seq"),
        P("seq"),
        P(),
    )
    return jax.shard_map(
        body, mesh=mesh, in_specs=placed, out_specs=P("seq", "head"), check_vma=False
    )
```

profile of v0, /device:TPU:0, one launch (start us, length us, event | category | flops | bytes accessed | tf_op | source)
XLA Modules:
  0.0 346.7 jit_solution(14417631467204702735)
XLA Ops:
  6.5 1.4 copy-done
  7.9 1.0 constant_dynamic-slice_fusion
  9.0 0.7 all-gather.11.cloned.1.call-update
  9.7 0.7 fusion.43
  10.4 102.7 %all-gather.7.cloned.1.call-done = bf16[3,4096,512]{2,1,0:T(8,128)(2,1)} async-done(((bf16[3,256,512]{2,1,0:T(8,128)(2,1)}), bf16[3,4096,512]{2,1,0:T(8,128)(2,1)}) %all-gather.7.cloned.1.call-update) | async-done | bytes 12582928 | tf_op jit(solution)/shard_map/all_gather | solution.py:49
  113.1 6.8 %fusion.23 = f32[128,512]{1,0:T(8,128)S(1)} fusion(bf16[3,4096,512]{2,1,0:T(8,128)(2,1)} %all-gather.7.cloned.1.call-done, bf16[128,3]{0,1:T(4,128)(2,1)S(1)} %fusion.43, bf16[128,4096]{1,0:T(8,128)(2,1)} %param.8), kind=kOutput, calls=%fused_computation.21 | convolution fusion | flops 1612185600 | bytes 13894400 | tf_op jit(solution)/shard_map/rsd,sdc->rc/dot_general | solution.py:46
  120.0 1.6 multiply_reduce_fusion.1
  121.6 119.7 %all-gather.11.cloned.1.call-done = bf16[3,4096,1024]{2,1,0:T(8,128)(2,1)} async-done(((bf16[3,256,1024]{2,1,0:T(8,128)(2,1)}), bf16[3,4096,1024]{2,1,0:T(8,128)(2,1)}) %all-gather.11.cloned.1.call-update) | async-done | bytes 25165840 | tf_op jit(solution)/shard_map/all_gather | solution.py:43
  241.4 10.6 %multiply_reduce_fusion = (f32[128]{0:T(128)}, f32[128,1024]{1,0:T(8,128)S(1)}) fusion(bf16[3,4096,1024]{2,1,0:T(8,128)(2,1)} %all-gather.11.cloned.1.call-done, bf16[128,3]{0,1:T(4,128)(2,1)S(1)} %fusion.43, bf16[128,4096]{1,0:T(8,128)(2,1)S(1)} %copy-done.1), kind=kOutput, calls=%fused_computation.30 | convolution fusion | flops 3223060480 | bytes 26739968 | tf_op jit(solution)/shard_map/rsd,sdc->rc/dot_general | solution.py:40
  252.0 5.0 %all-reduce = (f32[128]{0:T(128)S(1)}, f32[128]{0:T(128)S(1)}) all-reduce(f32[128]{0:T(128)} %get-tuple-element.5, f32[128]{0:T(128)} %get-tuple-element.9), channel_id=1, replica_groups=mesh['head'=2,'seq'=16] {'head'}, use_global_device_ids=true, to_apply=%region_2.3 | all-reduce | flops 256 | bytes 2048 | tf_op jit(solution)/shard_map/psum | solution.py:59
  257.4 0.6 copy.36
  258.1 0.7 select_reduce_fusion
  258.8 0.7 multiply_add_fusion
  259.5 20.3 %all-gather.1 = s32[16,1,128]{2,1,0:T(1,128)S(1)} all-gather(s32[1,1,128]{2,1,0:T(1,128)S(1)} %bitcast.67), channel_id=1, replica_groups=mesh['head'=2,'seq'=16] {'seq'}, dimensions={0}, use_global_device_ids=true | all-gather | bytes 8704 | tf_op jit(solution)/shard_map/all_gather | solution.py:75
  279.9 0.7 copy.27
  280.7 0.3 broadcast_compare_fusion
  281.1 1.2 fusion.22
  282.4 13.8 %all-gather.9.cloned.1.call-done = bf16[2048,2,128]{2,0,1:T(8,128)(2,1)} async-done(((bf16[128,2,128]{2,0,1:T(8,128)(2,1)}), bf16[2048,2,128]{2,0,1:T(8,128)(2,1)}) %all-gather.9.cloned.1.call-update) | async-done | bytes 1048592 | tf_op jit(solution)/shard_map/all_gather | solution.py:73
  296.2 2.6 fusion
  298.8 3.2 copy-done.2
  302.0 1.7 fusion.3
  303.7 30.3 %all-gather.13.cloned.1.call-done = bf16[2048,2,1,128]{0,3,1,2:T(8,128)(2,1)} async-done(((bf16[128,2,1,128]{0,3,1,2:T(8,128)(2,1)}), bf16[2048,2,1,128]{0,3,1,2:T(8,128)(2,1)}) %all-gather.13.cloned.1.call-update) | async-done | bytes 1048592 | tf_op jit(solution)/shard_map/all_gather | solution.py:74
  333.9 5.3 %fusion.36 = bf16[128,2,4,128]{0,3,2,1:T(8,128)(2,1)S(1)} fusion(f32[2,2048,128,4]{2,1,3,0:T(8,128)} %copy-done.2, f32[128,2,4]{0,2,1:T(4,128)S(1)} %broadcast_maximum_fusion, pred[128,2048]{0,1:T(8,128)(4,1)S(1)} %broadcast_compare_fusion, bf16[2048,2,1,128]{0,3,1,2:T(8,128)(2,1)} %all-gather.13.cloned.1.call-done, f32[128,2,4]{0,2,1:T(4,128)S(1)} %fusion.3), kind=kOutput, calls=%fused_computation.29 | convolution fusion | flops 545521664 | bytes 9969664 | tf_op jit(solution)/shard_map/rkgn,nkd->rkgd/dot_general | solution.py:84
  339.3 0.9 copy.23
  (22 shorter events, 1.0 us)
Async XLA Ops:
  6.5 1.4 copy-start
  6.5 106.5 %all-gather.7.cloned.1.call-start = ((), (), s32[]{:S(2)}) async-start(), calls=%async_computation | async-start | bytes 13369344 | tf_op jit(solution)/shard_map/all_gather | solution.py:49
  8.9 232.5 %all-gather.11.cloned.1.call-start = ((), (), s32[]{:S(2)}) async-start(), calls=%async_computation.2 | async-start | bytes 26738688 | tf_op jit(solution)/shard_map/all_gather | solution.py:43
  9.7 286.5 %all-gather.9.cloned.1.call-start = ((), (), s32[]{:S(2)}) async-start(), calls=%async_computation.1 | async-start | bytes 1114112 | tf_op jit(solution)/shard_map/all_gather | solution.py:73
  10.4 231.0 %copy-start.1 = (bf16[128,4096]{1,0:T(8,128)(2,1)S(1)}, bf16[128,4096]{1,0:T(8,128)(2,1)}, u32[]{:S(2)}) copy-start(bf16[128,4096]{1,0:T(8,128)(2,1)} %param.8) | copy-start | bytes 3145732
  121.6 135.5 %copy-start.3 = (s32[128]{0:T(128)S(1)}, s32[128]{0:T(128)}, u32[]{:S(2)}) copy-start(s32[128]{0:T(128)} %param.13) | copy-start | bytes 1540
  121.6 135.5 %copy-start.4 = (f32[3,512]{1,0:T(4,128)S(1)}, f32[3,512]{1,0:T(4,128)}, u32[]{:S(2)}) copy-start(f32[3,512]{1,0:T(4,128)} %param.12) | copy-start | bytes 18436
  258.0 75.9 %all-gather.13.cloned.1.call-start = ((), (), s32[]{:S(2)}) async-start(), calls=%async_computation.3 | async-start | bytes 1114112 | tf_op jit(solution)/shard_map/all_gather | solution.py:74
  298.8 3.2 copy-start.2
Sparse Core Ops, SparseCore 0:
  9.5 103.4 all-gather.6
  114.6 126.7 all-gather.10
  258.2 37.9 all-gather.8
  298.2 35.7 all-gather.12
where the time goes:
time: 347 us
  waiting for transfers between devices  267 us (77%)
  matrix products  26.7 us (8%)
  blocking collectives  25.3 us (7%)
  between operations  13.2 us (4%)
  local copies, waits for them, and re-layouts  8.27 us (2%)
  other arithmetic  5.75 us (2%)
    all_gather x1, waiting for transfers between devices, body(): lax.all_gather(w_query, 'seq', axis=1, tiled=True)  120 us
    all_gather x1, waiting for transfers between devices, body(): lax.all_gather(kv_weights, 'seq', axis=1, tiled=True)  103 us
    all_gather x1, waiting for transfers between devices, body(): value_part = lax.all_gather(values, 'seq', axis=0, tiled=True)  30.3 us
    all_gather x1, blocking collectives, body(): key_times = lax.all_gather(query_times, 'seq', axis=0, tiled=True)  20.3 us
    all_gather x1, waiting for transfers between devices, body(): key_part_now = lax.all_gather(k_normed, 'seq', axis=0, tiled=True)  13.8 us
    dot_general x1, matrix products, body(): jnp.einsum('rsd,sdc->rc', spread, lax.all_gather(w_query, 'seq', axis=1,...  10.6 us
  transfers between devices with their start and end apart: 4, of which 4 were waited for; matrix products, arithmetic and copies ran while one was open for 5% of the time, Pallas kernels for 0%

commit v1 on v0

v1 whole, which is shorter than its diff:
```python
import functools
import math

import jax
import jax.numpy as jnp
from jax import lax
from jax.experimental import pallas as pl
from jax.experimental.pallas import tpu as pltpu
from jax.sharding import PartitionSpec as P

HEADS = 16
KV_HEADS = 4
HEAD_DIM = 128
STREAMS = 3
FRAMES = 32
NEAR = 4
INFO = 8

epsilon = 1e-06
MIB = 1024 * 1024

VMEM = pl.BlockSpec(memory_space=pltpu.VMEM)
SMEM = pl.BlockSpec(memory_space=pltpu.SMEM)


def params(mib):
    return pltpu.CompilerParams(vmem_limit_bytes=mib * MIB)


def swap(x, mask):
    size = lax.axis_size("seq")
    return lax.ppermute(x, "seq", [(i, i ^ mask) for i in range(size)])


def head_sum(x):
    size = lax.axis_size("head")
    step = 1
    while step < size:
        x = x + lax.ppermute(x, "head", [(i, i ^ step) for i in range(size)])
        step *= 2
    return x


def to_row(column):
    return jnp.broadcast_to(column, (column.shape[0], 128)).T[:8]


def to_column(row):
    return jnp.broadcast_to(row, (128, row.shape[1])).T[:, :1]


def by_stream(ids, gain_ref, first, width):
    gain = jnp.zeros((ids.shape[0], width), jnp.float32)
    for s in range(STREAMS):
        gain = jnp.where(ids == s, gain_ref[s:s + 1, first:first + width], gain)
    return gain


def pack_kernel(far, me_ref, x_ref, info_ref, *out_refs):
    rows = x_ref.shape[0]
    width = x_ref.shape[1] // far
    me = me_ref[0] // NEAR
    info = info_ref[...].astype(jnp.bfloat16)
    for k in range(far):
        first = pl.multiple_of((me ^ k) * width, 128)
        out_refs[k][:rows] = x_ref[:, pl.ds(first, width)]
        out_refs[k][rows:, :rows] = info


def pack(x, info, me, far):
    rows, width = x.shape
    return pl.pallas_call(
        functools.partial(pack_kernel, far),
        out_shape=[jax.ShapeDtypeStruct((rows + INFO, width // far), x.dtype)] * far,
        in_specs=[SMEM, VMEM, VMEM],
        out_specs=[VMEM] * far,
        compiler_params=params(16),
        cost_estimate=pl.CostEstimate(flops=0, bytes_accessed=4 * rows * width, transcendentals=0),
        name="pack",
    )(me, x, info)


def project_kernel(far, rows, w_ref, *refs):
    x_refs, out_refs = refs[:far], refs[far:]
    x = jnp.concatenate([ref[:rows] for ref in x_refs], axis=0)
    ids = jnp.concatenate(
        [to_column(ref[rows:rows + 1, :rows].astype(jnp.float32)) for ref in x_refs], axis=0
    )
    total = None
    for s in range(STREAMS):
        chosen = jnp.where(ids == s, x, jnp.zeros_like(x))
        term = jnp.dot(chosen, w_ref[s], preferred_element_type=jnp.float32)
        total = term if total is None else total + term
    out_refs[0][...] = total[:rows]
    for k in range(1, far):
        out_refs[k][...] = total[k * rows:(k + 1) * rows].astype(jnp.bfloat16)


def project(x_parts, w):
    far = len(x_parts)
    padded, width = x_parts[0].shape
    rows = padded - INFO
    streams, depth, columns = w.shape
    tile = min(256, columns)
    shapes = [jax.ShapeDtypeStruct((rows, columns), jnp.float32)]
    shapes += [jax.ShapeDtypeStruct((rows, columns), jnp.bfloat16)] * (far - 1)
    return pl.pallas_call(
        functools.partial(project_kernel, far, rows),
        grid=(columns // tile,),
        out_shape=shapes,
        in_specs=[pl.BlockSpec((streams, depth, tile), lambda i: (0, 0, i))]
        + [pl.BlockSpec((padded, width), lambda i: (0, 0))] * far,
        out_specs=[pl.BlockSpec((rows, tile), lambda i: (0, i))] * far,
        compiler_params=params(24),
        cost_estimate=pl.CostEstimate(
            flops=2 * far * rows * width * streams * columns,
            bytes_accessed=2 * (far * rows * (width + columns) + streams * depth * columns),
            transcendentals=0,
        ),
        name="project",
    )(w, *x_parts)


def reduce_kernel(count, square_columns, *refs):
    part_refs, total_refs, square_ref = refs[:count], refs[count:-1], refs[-1]
    each = count // len(total_refs)
    squares = None
    for t, total_ref in enumerate(total_refs):
        total = part_refs[t * each][...]
        for ref in part_refs[t * each + 1:(t + 1) * each]:
            total = total + ref[...].astype(jnp.float32)
        total_ref[...] = total
        for first in range(0, total.shape[1], 2 * HEAD_DIM):
            block = total[:, first:first + square_columns]
            term = jnp.sum(block * block, axis=1, keepdims=True)
            squares = term if squares is None else squares + term
    square_ref[...] = to_row(squares)


def reduce(part_lists, square_columns):
    parts = [part for parts in part_lists for part in parts]
    shape = part_lists[0][0].shape
    return pl.pallas_call(
        functools.partial(reduce_kernel, len(parts), square_columns),
        out_shape=[jax.ShapeDtypeStruct(shape, jnp.float32)] * len(part_lists)
        + [jax.ShapeDtypeStruct((8, shape[0]), jnp.float32)],
        in_specs=[VMEM] * len(parts),
        out_specs=[VMEM] * (len(part_lists) + 1),
        compiler_params=params(16),
        cost_estimate=pl.CostEstimate(
            flops=2 * len(parts) * shape[0] * shape[1],
            bytes_accessed=3 * len(parts) * shape[0] * shape[1],
            transcendentals=0,
        ),
        name="reduce",
    )(*parts)


def normalize_kernel(total_ref, square_ref, gain_ref, x_ref, out_ref):
    rows = total_ref.shape[0]
    ids = to_column(x_ref[rows:rows + 1, :rows].astype(jnp.float32))
    scale = to_column(lax.rsqrt(square_ref[:1] / (KV_HEADS * HEAD_DIM) + epsilon))
    for g in range(gain_ref.shape[1] // HEAD_DIM):
        first = 2 * g * HEAD_DIM
        gain = by_stream(ids, gain_ref, g * HEAD_DIM, HEAD_DIM)
        key = total_ref[:, first:first + HEAD_DIM] * scale * gain
        out_ref[:, first:first + HEAD_DIM] = key.astype(jnp.bfloat16)
        value = total_ref[:, first + HEAD_DIM:first + 2 * HEAD_DIM]
        out_ref[:, first + HEAD_DIM:first + 2 * HEAD_DIM] = value.astype(jnp.bfloat16)


def normalize(total, squares, gain, x_own):
    return pl.pallas_call(
        normalize_kernel,
        out_shape=jax.ShapeDtypeStruct(total.shape, jnp.bfloat16),
        in_specs=[VMEM] * 4,
        out_specs=VMEM,
        compiler_params=params(16),
        cost_estimate=pl.CostEstimate(
            flops=4 * total.size, bytes_accessed=6 * total.size, transcendentals=0
        ),
        name="normalize",
    )(total, squares, gain, x_own)


def attend_kernel(kv_local, per_group, q_count, far, me_ref, map_ref, x_ref, square_ref, gain_ref,
                  *refs):
    q_refs, kv_refs, out_ref = refs[:q_count], refs[q_count:q_count + NEAR], refs[-1]
    rows, columns = q_refs[0].shape
    keys = far * rows
    kv_columns = kv_refs[0].shape[1]
    score_scale = 1.0 / math.sqrt(HEAD_DIM)
    me = me_ref[0]
    first_half = lax.broadcasted_iota(jnp.int32, (1, rows), 1) < rows // 2
    ids = to_column(x_ref[rows:rows + 1, :rows].astype(jnp.float32))
    q_scale = to_column(lax.rsqrt(square_ref[:1] / (HEADS * HEAD_DIM) + epsilon))

    key_times = []
    for j in range(NEAR):
        pieces = []
        for k in range(far):
            owner = me ^ (k * NEAR + j)
            row, lane = divmod(k * rows, kv_columns)
            local = kv_refs[j][keys + row:keys + row + 1, lane:lane + rows].astype(jnp.float32)
            block = jnp.where(first_half, map_ref[2 * owner], map_ref[2 * owner + 1])
            pieces.append((block * FRAMES).astype(jnp.float32) + local)
        key_times.append(jnp.concatenate(pieces, axis=1))
    query_times = to_column(key_times[0][:, :rows])

    for g in range(kv_local):
        for h in range(per_group):
            head = g * per_group + h
            chunk, first = divmod(head * HEAD_DIM, columns)
            gain = by_stream(ids, gain_ref, head * HEAD_DIM, HEAD_DIM)
            q = (q_refs[chunk][:, first:first + HEAD_DIM] * q_scale * gain).astype(jnp.bfloat16)
            scores = []
            for j in range(NEAR):
                key = kv_refs[j][:keys, 2 * g * HEAD_DIM:(2 * g + 1) * HEAD_DIM]
                score = lax.dot_general(
                    q, key, (((1,), (1,)), ((), ())), preferred_element_type=jnp.float32
                )
                scores.append(jnp.where(key_times[j] <= query_times, score * score_scale, -1e30))
            peak = functools.reduce(
                jnp.maximum, [jnp.max(s, axis=1, keepdims=True) for s in scores]
            )
            total = jnp.zeros((rows, 1), jnp.float32)
            mixed = jnp.zeros((rows, HEAD_DIM), jnp.float32)
            for j in range(NEAR):
                value = kv_refs[j][:keys, (2 * g + 1) * HEAD_DIM:(2 * g + 2) * HEAD_DIM]
                terms = jnp.exp(scores[j] - peak)
                total = total + jnp.sum(terms, axis=1, keepdims=True)
                mixed = mixed + jnp.dot(
                    terms.astype(jnp.bfloat16), value, preferred_element_type=jnp.float32
                )
            out = (mixed / total).astype(out_ref.dtype)
            out_ref[:, head * HEAD_DIM:(head + 1) * HEAD_DIM] = out


def attend(me, block_map, x_own, squares, q_gain, q_parts, kv_parts, far, kv_local, per_group):
    rows, columns = q_parts[0].shape
    keys = NEAR * far * rows
    count = rows * kv_local * per_group * keys
    return pl.pallas_call(
        functools.partial(attend_kernel, kv_local, per_group, len(q_parts), far),
        out_shape=jax.ShapeDtypeStruct((rows, columns * len(q_parts)), jnp.bfloat16),
        in_specs=[SMEM, SMEM] + [VMEM] * (3 + len(q_parts) + NEAR),
        out_specs=VMEM,
        compiler_params=params(40),
        cost_estimate=pl.CostEstimate(
            flops=4 * count * HEAD_DIM,
            bytes_accessed=4 * keys * kv_local * HEAD_DIM,
            transcendentals=count,
        ),
        name="attend",
    )(me, block_map, x_own, squares, q_gain, *q_parts, *kv_parts)


def body(activations, w_query, w_keyval, q_gain, k_gain, stream_ids, local_times, block_map):
    row_count = activations.shape[0]
    group_size = HEADS // KV_HEADS
    q_width = w_query.shape[2]
    q_local = q_width // HEAD_DIM
    per_group = min(group_size, q_local)
    kv_local = q_local // per_group
    replicas = max(1, lax.axis_size("head") // KV_HEADS)
    head_index = lax.axis_index("head")
    first_group = head_index * q_local // group_size
    size = lax.axis_size("seq")
    far = size // NEAR
    me = lax.axis_index("seq").reshape(1)

    info = jnp.pad(jnp.stack([stream_ids, local_times]), ((0, INFO - 2), (0, 0)))
    x_send = pack(activations, info, me, far)
    x_parts = [x_send[0]] + [swap(x_send[k], k * NEAR) for k in range(1, far)]

    groups = [[f * NEAR + j for j in range(NEAR)] for f in range(far)]

    def near_weights(w):
        return lax.all_gather(w, "seq", axis=1, tiled=True, axis_index_groups=groups)

    kv_weights = lax.dynamic_slice_in_dim(
        w_keyval, first_group * (2 * HEAD_DIM), kv_local * 2 * HEAD_DIM, 2
    )
    q_chunks = 2 if q_width % 512 == 0 else 1
    chunk = q_width // q_chunks

    def partial_sums(w):
        parts = project(x_parts, near_weights(w))
        return [parts[0]] + [swap(parts[k], k * NEAR) for k in range(1, far)]

    kv_total, key_sq = reduce([partial_sums(kv_weights)], HEAD_DIM)
    key_sq = head_sum(jnp.where(head_index % replicas == 0, key_sq, jnp.float32(0.0)))
    kv_gain = lax.dynamic_slice_in_dim(k_gain, first_group * HEAD_DIM, kv_local * HEAD_DIM, 1)
    kv_rows = normalize(kv_total, key_sq, kv_gain, x_parts[0])
    times = jnp.stack([part[row_count + 1, :row_count] for part in x_parts])
    times = times.reshape(-1, kv_rows.shape[1])
    times = jnp.pad(times, ((0, -times.shape[0] % 16), (0, 0)))
    kv_here = jnp.concatenate(
        [kv_rows] + [swap(kv_rows, k * NEAR) for k in range(1, far)] + [times]
    )
    kv_other = swap(kv_here, 2)
    kv_parts = [kv_here, swap(kv_here, 1), kv_other, swap(kv_other, 1)]

    q_parts = [partial_sums(w_query[:, :, c * chunk:(c + 1) * chunk]) for c in range(q_chunks)]
    *q_totals, query_sq = reduce(q_parts, 2 * HEAD_DIM)
    query_sq = head_sum(query_sq)
    return attend(
        me, block_map, x_parts[0], query_sq, q_gain, q_totals, kv_parts, far, kv_local, per_group
    )


def solution(mesh):
    placed = (
        P("seq", None),
        P(None, "seq", "head"),
        P(None, "seq", None),
        P(None, "head"),
        P(),
        P("seq"),
        P("seq"),
        P(),
    )
    return jax.shard_map(
        body, mesh=mesh, in_specs=placed, out_specs=P("seq", "head"), check_vma=False
    )
```

time: 347 us -> 153 us (0.44)
  waiting for transfers between devices: 267 us -> 76.8 us
  starting transfers between devices: 0.12 us -> 32 us
  matrix products: 26.7 us -> 0 us
  blocking collectives: 25.3 us -> 0 us
  Pallas kernels: 0 us -> 17.1 us
  other arithmetic: 5.75 us -> 0.03 us
  local copies, waits for them, and re-layouts: 8.27 us -> 12.8 us
    all_gather x4 -> x3, waiting for transfers between devices: 266 us -> 3.18 us  [near_weights(): lax.all_gather(w, 'seq', axis=1, tiled=True, axis_index_groups=groups)]
    ppermute x0 -> x20, waiting for transfers between devices: none -> 72.9 us  [the longest x18 69.2 us: swap(): return lax.ppermute(x, 'seq', [(i, i ^ mask) for i in range(size)])]
    ppermute x0 -> x20, starting transfers between devices: none -> 31.9 us  [the longest x18 27.7 us: swap(): return lax.ppermute(x, 'seq', [(i, i ^ mask) for i in range(size)])]
    dot_general x6 -> x0, matrix products: 26.7 us -> none  [the longest x1 10.6 us: body(): jnp.einsum('rsd,sdc->rc', spread, lax.all_gather(w_query, 'seq', axis=1,...]
    all_gather x1 -> x0, blocking collectives: 20.3 us -> none  [body(): key_times = lax.all_gather(query_times, 'seq', axis=0, tiled=True)]
    pallas_call x0 -> x8, Pallas kernels: none -> 17.1 us  [the longest x3 9.87 us: project(): pl.pallas_call(functools.partial(project_kernel, far, rows), grid=(column...]
    unnamed x11 -> x39, local copies, waits for them, and re-layouts: 5.34 us -> 10.5 us
    psum x1 -> x0, blocking collectives: 5.05 us -> none  [body(): lax.psum((jnp.sum(query_sum * query_sum, axis=1), key_part), 'head')]
  transfers between devices with their start and end apart: 4 -> 23, of which waited for: 4 -> 13; matrix products, arithmetic and copies ran while one was open for 5% -> 1% of each run, Pallas kernels for 0% -> 7%
where the time goes in v1:
time: 153 us; the launch traced here: 152 us
  waiting for transfers between devices  76.8 us (50%)
  starting transfers between devices  32 us (21%)
  Pallas kernels  17.1 us (11%)
  between operations  13.3 us (9%)
  local copies, waits for them, and re-layouts  12.8 us (8%)
    ppermute x18, waiting for transfers between devices, swap(): return lax.ppermute(x, 'seq', [(i, i ^ mask) for i in range(size)])  69.2 us
    ppermute x18, starting transfers between devices, swap(): return lax.ppermute(x, 'seq', [(i, i ^ mask) for i in range(size)])  27.7 us
    unnamed x39, local copies, waits for them, and re-layouts  10.5 us
    pallas_call x3, Pallas kernels, project(): pl.pallas_call(functools.partial(project_kernel, far, rows), grid=(column...  9.87 us
    pallas_call x1, Pallas kernels, attend(): pl.pallas_call(functools.partial(attend_kernel, kv_local, per_group, len(...  6.58 us
    ppermute x2, starting transfers between devices, head_sum(): x = x + lax.ppermute(x, 'head', [(i, i ^ step) for i in range(size)])  4.23 us
    ppermute x2, waiting for transfers between devices, head_sum(): x = x + lax.ppermute(x, 'head', [(i, i ^ step) for i in range(size)])  3.66 us
    all_gather x3, waiting for transfers between devices, near_weights(): lax.all_gather(w, 'seq', axis=1, tiled=True, axis_index_groups=groups)  3.18 us
  transfers between devices with their start and end apart: 23, of which 13 were waited for; matrix products, arithmetic and copies ran while one was open for 1% of the time, Pallas kernels for 7%

profile of v1, /device:TPU:0, one launch (start us, length us, event | category | flops | bytes accessed | tf_op | source)
XLA Modules:
  0.0 152.0 jit_solution(650055213967115437)
XLA Ops:
  11.6 3.1 %collective-permute-start = (bf16[136,1024]{1,0:T(8,128)(2,1)S(1)}, bf16[136,1024]{1,0:T(8,128)(2,1)S(1)}, u32[]{:S(2)}, u32[]{:S(2)}) collective-permute-start(bf16[136,1024]{1,0:T(8,128)(2,1)S(1)} %get-tuple-element.27), channel_id=1, source_target_pairs={{0,4},{1,5},{2,6},{3,7},{4,0},{5,1},{6,2},{7,3},{8,12},{9,13},{10,... | collective-permute-start | bytes 835592 | tf_op jit(solution)/shard_map/ppermute | solution.py:32
  14.7 2.6 %collective-permute-start.1 = (bf16[136,1024]{1,0:T(8,128)(2,1)S(1)}, bf16[136,1024]{1,0:T(8,128)(2,1)S(1)}, u32[]{:S(2)}, u32[]{:S(2)}) collective-permute-start(bf16[136,1024]{1,0:T(8,128)(2,1)S(1)} %get-tuple-element.28), channel_id=1, source_target_pairs={{0,8},{1,9},{2,10},{3,11},{4,12},{5,13},{6,14},{7,15},{8,0},{9,1},... | collective-permute-start | bytes 835592 | tf_op jit(solution)/shard_map/ppermute | solution.py:32
  17.3 9.3 %collective-permute-done.refs_1_ = bf16[136,1024]{1,0:T(8,128)(2,1)S(1)} collective-permute-done((bf16[136,1024]{1,0:T(8,128)(2,1)S(1)}, bf16[136,1024]{1,0:T(8,128)(2,1)S(1)}, u32[]{:S(2)}, u32[]{:S(2)}) %collective-permute-start) | collective-permute-done | bytes 278560 | tf_op jit(solution)/shard_map/ppermute | solution.py:32
  26.6 10.6 %collective-permute-done.1.refs_2_ = bf16[136,1024]{1,0:T(8,128)(2,1)S(1)} collective-permute-done((bf16[136,1024]{1,0:T(8,128)(2,1)S(1)}, bf16[136,1024]{1,0:T(8,128)(2,1)S(1)}, u32[]{:S(2)}, u32[]{:S(2)}) %collective-permute-start.1) | collective-permute-done | bytes 278560 | tf_op jit(solution)/shard_map/ppermute | solution.py:32
  37.1 3.2 %all-gather.8.cloned.1.call-done.w_ref = bf16[3,1024,512]{2,1,0:T(8,128)(2,1)} async-done(((bf16[3,256,512]{2,1,0:T(8,128)(2,1)}), bf16[3,1024,512]{2,1,0:T(8,128)(2,1)}) %all-gather.8.cloned.1.call-update) | async-done | bytes 3145744 | tf_op jit(solution)/shard_map/all_gather | solution.py:279
  40.3 1.9 %copy-done.4 = bf16[3,1024,512]{2,1,0:T(8,128)(2,1)S(1)} copy-done((bf16[3,1024,512]{2,1,0:T(8,128)(2,1)S(1)}, bf16[3,1024,512]{2,1,0:T(8,128)(2,1)}, u32[]{:S(2)}) %copy-start.4) | copy-done | bytes 3145752
  42.2 3.5 %project.5 = (f32[128,512]{1,0:T(8,128)S(1)}, bf16[128,512]{1,0:T(8,128)(2,1)}, bf16[128,512]{1,0:T(8,128)(2,1)}, bf16[128,512]{1,0:T(8,128)(2,1)}) custom-call(bf16[3,1024,512]{2,1,0:T(8,128)(2,1)S(1)} %copy-done.4, bf16[136,1024]{1,0:T(8,128)(2,1)S(1)} %get-tuple-element.26.refs_0_.x_ref, bf16[136,1024]{1,0:T(8,128)(2,1)S(1)} %collective-permute-done.refs_1_, ...), custom_call_target="tpu_custom_call" | custom-call | flops 1610612736 | bytes 4718592 | tf_op jit(solution)/shard_map/project/pallas_call | solution.py:107
  45.7 2.0 %collective-permute-start.10 = (bf16[128,512]{1,0:T(8,128)(2,1)}, bf16[128,512]{1,0:T(8,128)(2,1)S(1)}, u32[]{:S(2)}, u32[]{:S(2)}) collective-permute-start(bf16[128,512]{1,0:T(8,128)(2,1)} %get-tuple-element.42), channel_id=1, source_target_pairs={{0,4},{1,5},{2,6},{3,7},{4,0},{5,1},{6,2},{7,3},{8,12},{9,13},{10,... | collective-permute-start | bytes 393224 | tf_op jit(solution)/shard_map/ppermute | solution.py:32
  50.2 2.9 %collective-permute-done.10.refs_1_ = bf16[128,512]{1,0:T(8,128)(2,1)S(1)} collective-permute-done((bf16[128,512]{1,0:T(8,128)(2,1)}, bf16[128,512]{1,0:T(8,128)(2,1)S(1)}, u32[]{:S(2)}, u32[]{:S(2)}) %collective-permute-start.10) | collective-permute-done | bytes 131104 | tf_op jit(solution)/shard_map/ppermute | solution.py:32
  53.1 7.6 %collective-permute-done.11.refs_2_ = bf16[128,512]{1,0:T(8,128)(2,1)S(1)} collective-permute-done((bf16[128,512]{1,0:T(8,128)(2,1)}, bf16[128,512]{1,0:T(8,128)(2,1)S(1)}, u32[]{:S(2)}, u32[]{:S(2)}) %collective-permute-start.11) | collective-permute-done | bytes 131104 | tf_op jit(solution)/shard_map/ppermute | solution.py:32
  62.4 2.1 %collective-permute-done.13 = f32[8,128]{1,0:T(8,128)S(1)} collective-permute-done((f32[8,128]{1,0:T(8,128)S(1)}, f32[8,128]{1,0:T(8,128)S(1)}, u32[]{:S(2)}, u32[]{:S(2)}) %collective-permute-start.13) | collective-permute-done | bytes 4128 | tf_op jit(solution)/shard_map/ppermute | solution.py:39
  64.7 2.1 %collective-permute-start.14 = (bf16[128,512]{1,0:T(8,128)(2,1)S(1)}, bf16[128,512]{1,0:T(8,128)(2,1)S(1)}, u32[]{:S(2)}, u32[]{:S(2)}) collective-permute-start(bf16[128,512]{1,0:T(8,128)(2,1)S(1)} %normalize.1), channel_id=1, source_target_pairs={{0,4},{1,5},{2,6},{3,7},{4,0},{5,1},{6,2},{7,3},{8,12},{9,13},{10,... | collective-permute-start | bytes 393224 | tf_op jit(solution)/shard_map/ppermute | solution.py:32
  70.8 7.2 %collective-permute-done.15 = bf16[128,512]{1,0:T(8,128)(2,1)S(1)} collective-permute-done((bf16[128,512]{1,0:T(8,128)(2,1)S(1)}, bf16[128,512]{1,0:T(8,128)(2,1)S(1)}, u32[]{:S(2)}, u32[]{:S(2)}) %collective-permute-start.15) | collective-permute-done | bytes 131104 | tf_op jit(solution)/shard_map/ppermute | solution.py:32
  78.4 20.1 %collective-permute-done.18.refs_4_ = bf16[528,512]{1,0:T(8,128)(2,1)} collective-permute-done((bf16[528,512]{1,0:T(8,128)(2,1)S(1)}, bf16[528,512]{1,0:T(8,128)(2,1)}, u32[]{:S(2)}, u32[]{:S(2)}) %collective-permute-start.18) | collective-permute-done | bytes 540704 | tf_op jit(solution)/shard_map/ppermute | solution.py:32
  98.6 1.9 %copy-done.3 = bf16[3,1024,512]{2,1,0:T(8,128)(2,1)S(1)} copy-done((bf16[3,1024,512]{2,1,0:T(8,128)(2,1)S(1)}, bf16[3,1024,512]{2,1,0:T(8,128)(2,1)}, u32[]{:S(2)}) %copy-start.3) | copy-done | bytes 3145752
  101.4 3.5 %project.3 = (f32[128,512]{1,0:T(8,128)S(1)}, bf16[128,512]{1,0:T(8,128)(2,1)}, bf16[128,512]{1,0:T(8,128)(2,1)}, bf16[128,512]{1,0:T(8,128)(2,1)}) custom-call(bf16[3,1024,512]{2,1,0:T(8,128)(2,1)S(1)} %copy-done.3, bf16[136,1024]{1,0:T(8,128)(2,1)S(1)} %get-tuple-element.26.refs_0_.x_ref, bf16[136,1024]{1,0:T(8,128)(2,1)S(1)} %collective-permute-done.refs_1_, ...), custom_call_target="tpu_custom_call" | custom-call | flops 1610612736 | bytes 4718592 | tf_op jit(solution)/shard_map/project/pallas_call | solution.py:107
  104.9 5.7 %collective-permute-start.3 = (bf16[128,512]{1,0:T(8,128)(2,1)}, bf16[128,512]{1,0:T(8,128)(2,1)S(1)}, u32[]{:S(2)}, u32[]{:S(2)}) collective-permute-start(bf16[128,512]{1,0:T(8,128)(2,1)} %get-tuple-element.31), channel_id=1, source_target_pairs={{0,4},{1,5},{2,6},{3,7},{4,0},{5,1},{6,2},{7,3},{8,12},{9,13},{10,... | collective-permute-start | bytes 393224 | tf_op jit(solution)/shard_map/ppermute | solution.py:32
  113.9 1.9 %copy-done.2 = bf16[3,1024,512]{2,1,0:T(8,128)(2,1)S(1)} copy-done((bf16[3,1024,512]{2,1,0:T(8,128)(2,1)S(1)}, bf16[3,1024,512]{2,1,0:T(8,128)(2,1)}, u32[]{:S(2)}) %copy-start.2) | copy-done | bytes 3145752
  117.7 2.8 %project.4 = (f32[128,512]{1,0:T(8,128)S(1)}, bf16[128,512]{1,0:T(8,128)(2,1)S(1)}, bf16[128,512]{1,0:T(8,128)(2,1)S(1)}, bf16[128,512]{1,0:T(8,128)(2,1)S(1)}) custom-call(bf16[3,1024,512]{2,1,0:T(8,128)(2,1)S(1)} %copy-done.2, bf16[136,1024]{1,0:T(8,128)(2,1)S(1)} %get-tuple-element.26.refs_0_.x_ref, bf16[136,1024]{1,0:T(8,128)(2,1)S(1)} %collective-permute-done.refs_1_, ...), custom_call_target="tpu_custom_call" | custom-call | flops 1610612736 | bytes 4718592 | tf_op jit(solution)/shard_map/project/pallas_call | solution.py:107
  121.2 2.6 %collective-permute-done.4.refs_2_ = bf16[128,512]{1,0:T(8,128)(2,1)S(1)} collective-permute-done((bf16[128,512]{1,0:T(8,128)(2,1)}, bf16[128,512]{1,0:T(8,128)(2,1)S(1)}, u32[]{:S(2)}, u32[]{:S(2)}) %collective-permute-start.4) | collective-permute-done | bytes 131104 | tf_op jit(solution)/shard_map/ppermute | solution.py:32
  123.8 3.0 %collective-permute-start.8 = (bf16[128,512]{1,0:T(8,128)(2,1)S(1)}, bf16[128,512]{1,0:T(8,128)(2,1)S(1)}, u32[]{:S(2)}, u32[]{:S(2)}) collective-permute-start(bf16[128,512]{1,0:T(8,128)(2,1)S(1)} %get-tuple-element.37), channel_id=1, source_target_pairs={{0,12},{1,13},{2,14},{3,15},{4,8},{5,9},{6,10},{7,11},{8,4},{9,5},... | collective-permute-start | bytes 393224 | tf_op jit(solution)/shard_map/ppermute | solution.py:32
  127.9 6.4 %collective-permute-done.7.refs_6_ = bf16[128,512]{1,0:T(8,128)(2,1)S(1)} collective-permute-done((bf16[128,512]{1,0:T(8,128)(2,1)S(1)}, bf16[128,512]{1,0:T(8,128)(2,1)S(1)}, u32[]{:S(2)}, u32[]{:S(2)}) %collective-permute-start.7) | collective-permute-done | bytes 131104 | tf_op jit(solution)/shard_map/ppermute | solution.py:32
  134.6 2.7 %collective-permute-start.9 = (f32[8,128]{1,0:T(8,128)S(1)}, f32[8,128]{1,0:T(8,128)S(1)}, u32[]{:S(2)}, u32[]{:S(2)}) collective-permute-start(f32[8,128]{1,0:T(8,128)S(1)} %get-tuple-element.38), channel_id=1, source_target_pairs={{0,16},{16,0},{1,17},{17,1},{2,18},{18,2},{3,19},{19,3},{4,20},{20... | collective-permute-start | bytes 12296 | tf_op jit(solution)/shard_map/ppermute | solution.py:39
  138.9 6.6 %attend.1 = bf16[128,1024]{1,0:T(8,128)(2,1)} custom-call(s32[1]{0:T(128)} %bitcast.me_ref, s32[32]{0:T(128)S(1)} %copy-done.12, bf16[136,1024]{1,0:T(8,128)(2,1)S(1)} %get-tuple-element.26.refs_0_.x_ref, f32[8,128]{1,0:T(8,128)S(1)} %add.19.square_ref, f32[3,1024]{1,0:T(4,128)S(1)} %copy-done.11, f32[128,512]{1,0:T(8,128)S(1)} %get-tuple-element.39.refs_0_, ...), custom_call_target="tpu_custom_call" | custom-call | flops 1073741824 | bytes 2097152 | tf_op jit(solution)/shard_map/attend/pallas_call | solution.py:243
  (85 shorter events, 23.5 us)
Async XLA Ops:
  6.5 33.8 %all-gather.8.cloned.1.call-start = ((), (), s32[]{:S(2)}) async-start(), calls=%async_computation.2 | async-start | bytes 3932160 | tf_op jit(solution)/shard_map/all_gather | solution.py:279
  8.9 89.6 %all-gather.4.cloned.1.call-start = ((), (), s32[]{:S(2)}) async-start(), calls=%async_computation | async-start | bytes 3932160 | tf_op jit(solution)/shard_map/all_gather | solution.py:279
  10.3 103.6 %all-gather.6.cloned.1.call-start = ((), (), s32[]{:S(2)}) async-start(), calls=%async_computation.1 | async-start | bytes 3932160 | tf_op jit(solution)/shard_map/all_gather | solution.py:279
  11.6 14.9 %collective-permute-start = (bf16[136,1024]{1,0:T(8,128)(2,1)S(1)}, bf16[136,1024]{1,0:T(8,128)(2,1)S(1)}, u32[]{:S(2)}, u32[]{:S(2)}) collective-permute-start(bf16[136,1024]{1,0:T(8,128)(2,1)S(1)} %get-tuple-element.27), channel_id=1, source_target_pairs={{0,4},{1,5},{2,6},{3,7},{4,0},{5,1},{6,2},{7,3},{8,12},{9,13},{10,... | collective-permute-start | bytes 835592 | tf_op jit(solution)/shard_map/ppermute | solution.py:32
  14.7 22.4 %collective-permute-start.1 = (bf16[136,1024]{1,0:T(8,128)(2,1)S(1)}, bf16[136,1024]{1,0:T(8,128)(2,1)S(1)}, u32[]{:S(2)}, u32[]{:S(2)}) collective-permute-start(bf16[136,1024]{1,0:T(8,128)(2,1)S(1)} %get-tuple-element.28), channel_id=1, source_target_pairs={{0,8},{1,9},{2,10},{3,11},{4,12},{5,13},{6,14},{7,15},{8,0},{9,1},... | collective-permute-start | bytes 835592 | tf_op jit(solution)/shard_map/ppermute | solution.py:32
  17.3 19.8 %collective-permute-start.2 = (bf16[136,1024]{1,0:T(8,128)(2,1)S(1)}, bf16[136,1024]{1,0:T(8,128)(2,1)S(1)}, u32[]{:S(2)}, u32[]{:S(2)}) collective-permute-start(bf16[136,1024]{1,0:T(8,128)(2,1)S(1)} %get-tuple-element.29), channel_id=1, source_target_pairs={{0,12},{1,13},{2,14},{3,15},{4,8},{5,9},{6,10},{7,11},{8,4},{9,5},... | collective-permute-start | bytes 835592 | tf_op jit(solution)/shard_map/ppermute | solution.py:32
  45.7 7.4 %collective-permute-start.10 = (bf16[128,512]{1,0:T(8,128)(2,1)}, bf16[128,512]{1,0:T(8,128)(2,1)S(1)}, u32[]{:S(2)}, u32[]{:S(2)}) collective-permute-start(bf16[128,512]{1,0:T(8,128)(2,1)} %get-tuple-element.42), channel_id=1, source_target_pairs={{0,4},{1,5},{2,6},{3,7},{4,0},{5,1},{6,2},{7,3},{8,12},{9,13},{10,... | collective-permute-start | bytes 393224 | tf_op jit(solution)/shard_map/ppermute | solution.py:32
  47.8 13.0 %collective-permute-start.11 = (bf16[128,512]{1,0:T(8,128)(2,1)}, bf16[128,512]{1,0:T(8,128)(2,1)S(1)}, u32[]{:S(2)}, u32[]{:S(2)}) collective-permute-start(bf16[128,512]{1,0:T(8,128)(2,1)} %get-tuple-element.43), channel_id=1, source_target_pairs={{0,8},{1,9},{2,10},{3,11},{4,12},{5,13},{6,14},{7,15},{8,0},{9,1},... | collective-permute-start | bytes 393224 | tf_op jit(solution)/shard_map/ppermute | solution.py:32
  49.6 11.1 %collective-permute-start.12 = (bf16[128,512]{1,0:T(8,128)(2,1)}, bf16[128,512]{1,0:T(8,128)(2,1)S(1)}, u32[]{:S(2)}, u32[]{:S(2)}) collective-permute-start(bf16[128,512]{1,0:T(8,128)(2,1)} %get-tuple-element.44), channel_id=1, source_target_pairs={{0,12},{1,13},{2,14},{3,15},{4,8},{5,9},{6,10},{7,11},{8,4},{9,5},... | collective-permute-start | bytes 393224 | tf_op jit(solution)/shard_map/ppermute | solution.py:32
  60.9 3.6 %collective-permute-start.13 = (f32[8,128]{1,0:T(8,128)S(1)}, f32[8,128]{1,0:T(8,128)S(1)}, u32[]{:S(2)}, u32[]{:S(2)}) collective-permute-start(f32[8,128]{1,0:T(8,128)S(1)} %get-tuple-element.46), channel_id=1, source_target_pairs={{0,16},{16,0},{1,17},{17,1},{2,18},{18,2},{3,19},{19,3},{4,20},{20... | collective-permute-start | bytes 12296 | tf_op jit(solution)/shard_map/ppermute | solution.py:39
  62.4 36.1 %copy-start.6 = (bf16[136,1024]{1,0:T(8,128)(2,1)S(1)}, bf16[136,1024]{1,0:T(8,128)(2,1)}, u32[]{:S(2)}) copy-start(bf16[136,1024]{1,0:T(8,128)(2,1)} %copy-done.5) | copy-start | bytes 835588
  64.7 6.0 %collective-permute-start.14 = (bf16[128,512]{1,0:T(8,128)(2,1)S(1)}, bf16[128,512]{1,0:T(8,128)(2,1)S(1)}, u32[]{:S(2)}, u32[]{:S(2)}) collective-permute-start(bf16[128,512]{1,0:T(8,128)(2,1)S(1)} %normalize.1), channel_id=1, source_target_pairs={{0,4},{1,5},{2,6},{3,7},{4,0},{5,1},{6,2},{7,3},{8,12},{9,13},{10,... | collective-permute-start | bytes 393224 | tf_op jit(solution)/shard_map/ppermute | solution.py:32
  66.8 11.2 %collective-permute-start.15 = (bf16[128,512]{1,0:T(8,128)(2,1)S(1)}, bf16[128,512]{1,0:T(8,128)(2,1)S(1)}, u32[]{:S(2)}, u32[]{:S(2)}) collective-permute-start(bf16[128,512]{1,0:T(8,128)(2,1)S(1)} %normalize.1), channel_id=1, source_target_pairs={{0,8},{1,9},{2,10},{3,11},{4,12},{5,13},{6,14},{7,15},{8,0},{9,1},... | collective-permute-start | bytes 393224 | tf_op jit(solution)/shard_map/ppermute | solution.py:32
  67.8 10.2 %collective-permute-start.16 = (bf16[128,512]{1,0:T(8,128)(2,1)S(1)}, bf16[128,512]{1,0:T(8,128)(2,1)S(1)}, u32[]{:S(2)}, u32[]{:S(2)}) collective-permute-start(bf16[128,512]{1,0:T(8,128)(2,1)S(1)} %normalize.1), channel_id=1, source_target_pairs={{0,12},{1,13},{2,14},{3,15},{4,8},{5,9},{6,10},{7,11},{8,4},{9,5},... | collective-permute-start | bytes 393224 | tf_op jit(solution)/shard_map/ppermute | solution.py:32
  78.1 20.5 %collective-permute-start.18 = (bf16[528,512]{1,0:T(8,128)(2,1)S(1)}, bf16[528,512]{1,0:T(8,128)(2,1)}, u32[]{:S(2)}, u32[]{:S(2)}) collective-permute-start(bf16[528,512]{1,0:T(8,128)(2,1)S(1)} %pad_dynamic-update-slice_fusion.refs_2_), channel_id=1, source_target_pairs={{0,2},{1,3},{2,0},{3,1},{4,6},{5,7},{6,4},{7,5},{8,10},{9,11},{10,... | collective-permute-start | bytes 1622024 | tf_op jit(solution)/shard_map/ppermute | solution.py:32
  78.4 60.5 %collective-permute-start.17 = (bf16[528,512]{1,0:T(8,128)(2,1)S(1)}, bf16[528,512]{1,0:T(8,128)(2,1)}, u32[]{:S(2)}, u32[]{:S(2)}) collective-permute-start(bf16[528,512]{1,0:T(8,128)(2,1)S(1)} %pad_dynamic-update-slice_fusion.refs_2_), channel_id=1, source_target_pairs={{0,1},{1,0},{2,3},{3,2},{4,5},{5,4},{6,7},{7,6},{8,9},{9,8},{10,11... | collective-permute-start | bytes 1622024 | tf_op jit(solution)/shard_map/ppermute | solution.py:32
  98.6 40.3 %collective-permute-start.19 = (bf16[528,512]{1,0:T(8,128)(2,1)}, bf16[528,512]{1,0:T(8,128)(2,1)}, u32[]{:S(2)}, u32[]{:S(2)}) collective-permute-start(bf16[528,512]{1,0:T(8,128)(2,1)} %collective-permute-done.18.refs_4_), channel_id=1, source_target_pairs={{0,1},{1,0},{2,3},{3,2},{4,5},{5,4},{6,7},{7,6},{8,9},{9,8},{10,11... | collective-permute-start | bytes 1622024 | tf_op jit(solution)/shard_map/ppermute | solution.py:32
  104.9 15.6 %collective-permute-start.3 = (bf16[128,512]{1,0:T(8,128)(2,1)}, bf16[128,512]{1,0:T(8,128)(2,1)S(1)}, u32[]{:S(2)}, u32[]{:S(2)}) collective-permute-start(bf16[128,512]{1,0:T(8,128)(2,1)} %get-tuple-element.31), channel_id=1, source_target_pairs={{0,4},{1,5},{2,6},{3,7},{4,0},{5,1},{6,2},{7,3},{8,12},{9,13},{10,... | collective-permute-start | bytes 393224 | tf_op jit(solution)/shard_map/ppermute | solution.py:32
  110.7 13.1 %collective-permute-start.4 = (bf16[128,512]{1,0:T(8,128)(2,1)}, bf16[128,512]{1,0:T(8,128)(2,1)S(1)}, u32[]{:S(2)}, u32[]{:S(2)}) collective-permute-start(bf16[128,512]{1,0:T(8,128)(2,1)} %get-tuple-element.32), channel_id=1, source_target_pairs={{0,8},{1,9},{2,10},{3,11},{4,12},{5,13},{6,14},{7,15},{8,0},{9,1},... | collective-permute-start | bytes 393224 | tf_op jit(solution)/shard_map/ppermute | solution.py:32
  112.4 11.4 %collective-permute-start.5 = (bf16[128,512]{1,0:T(8,128)(2,1)}, bf16[128,512]{1,0:T(8,128)(2,1)S(1)}, u32[]{:S(2)}, u32[]{:S(2)}) collective-permute-start(bf16[128,512]{1,0:T(8,128)(2,1)} %get-tuple-element.33), channel_id=1, source_target_pairs={{0,12},{1,13},{2,14},{3,15},{4,8},{5,9},{6,10},{7,11},{8,4},{9,5},... | collective-permute-start | bytes 393224 | tf_op jit(solution)/shard_map/ppermute | solution.py:32
  120.5 7.4 %collective-permute-start.6 = (bf16[128,512]{1,0:T(8,128)(2,1)S(1)}, bf16[128,512]{1,0:T(8,128)(2,1)S(1)}, u32[]{:S(2)}, u32[]{:S(2)}) collective-permute-start(bf16[128,512]{1,0:T(8,128)(2,1)S(1)} %get-tuple-element.35), channel_id=1, source_target_pairs={{0,4},{1,5},{2,6},{3,7},{4,0},{5,1},{6,2},{7,3},{8,12},{9,13},{10,... | collective-permute-start | bytes 393224 | tf_op jit(solution)/shard_map/ppermute | solution.py:32
  123.8 10.5 %collective-permute-start.7 = (bf16[128,512]{1,0:T(8,128)(2,1)S(1)}, bf16[128,512]{1,0:T(8,128)(2,1)S(1)}, u32[]{:S(2)}, u32[]{:S(2)}) collective-permute-start(bf16[128,512]{1,0:T(8,128)(2,1)S(1)} %get-tuple-element.36), channel_id=1, source_target_pairs={{0,8},{1,9},{2,10},{3,11},{4,12},{5,13},{6,14},{7,15},{8,0},{9,1},... | collective-permute-start | bytes 393224 | tf_op jit(solution)/shard_map/ppermute | solution.py:32
  123.8 10.5 %collective-permute-start.8 = (bf16[128,512]{1,0:T(8,128)(2,1)S(1)}, bf16[128,512]{1,0:T(8,128)(2,1)S(1)}, u32[]{:S(2)}, u32[]{:S(2)}) collective-permute-start(bf16[128,512]{1,0:T(8,128)(2,1)S(1)} %get-tuple-element.37), channel_id=1, source_target_pairs={{0,12},{1,13},{2,14},{3,15},{4,8},{5,9},{6,10},{7,11},{8,4},{9,5},... | collective-permute-start | bytes 393224 | tf_op jit(solution)/shard_map/ppermute | solution.py:32
  134.6 4.3 %collective-permute-start.9 = (f32[8,128]{1,0:T(8,128)S(1)}, f32[8,128]{1,0:T(8,128)S(1)}, u32[]{:S(2)}, u32[]{:S(2)}) collective-permute-start(f32[8,128]{1,0:T(8,128)S(1)} %get-tuple-element.38), channel_id=1, source_target_pairs={{0,16},{16,0},{1,17},{17,1},{2,18},{18,2},{3,19},{19,3},{4,20},{20... | collective-permute-start | bytes 12296 | tf_op jit(solution)/shard_map/ppermute | solution.py:39
  (16 other events, 133.6 us)
Sparse Core Ops, SparseCore 0:
  9.1 31.2 all-gather.7
  41.9 28.5 all-gather.3
  72.0 33.9 all-gather.5

commit v2 on v1

v2 whole, which is shorter than its diff:
```python
import functools
import math

import jax
import jax.numpy as jnp
from jax import lax
from jax.experimental import pallas as pl
from jax.experimental.pallas import tpu as pltpu
from jax.sharding import PartitionSpec as P

HEADS = 16
KV_HEADS = 4
HEAD_DIM = 128
STREAMS = 3
FRAMES = 32
NEAR = 4
INFO = 8

epsilon = 1e-06
MIB = 1024 * 1024

VMEM = pl.BlockSpec(memory_space=pltpu.VMEM)
SMEM = pl.BlockSpec(memory_space=pltpu.SMEM)


def params(mib):
    return pltpu.CompilerParams(vmem_limit_bytes=mib * MIB)


def swap(x, mask):
    size = lax.axis_size("seq")
    return lax.ppermute(x, "seq", [(i, i ^ mask) for i in range(size)])


def after(x, *others):
    return lax.optimization_barrier((x,) + others)[0]


def head_sum(x):
    size = lax.axis_size("head")
    step = 1
    while step < size:
        x = x + lax.ppermute(x, "head", [(i, i ^ step) for i in range(size)])
        step *= 2
    return x


def to_row(column):
    return jnp.broadcast_to(column, (column.shape[0], 128)).T[:8]


def to_column(row):
    return jnp.broadcast_to(row, (128, row.shape[1])).T[:, :1]


def by_stream(ids, gain_ref, first, width):
    gain = jnp.zeros((ids.shape[0], width), jnp.float32)
    for s in range(STREAMS):
        gain = jnp.where(ids == s, gain_ref[s:s + 1, first:first + width], gain)
    return gain


def pack_kernel(far, me_ref, x_ref, info_ref, out_ref):
    rows = x_ref.shape[0]
    depth = x_ref.shape[1] // (far * NEAR)
    near = me_ref[0] % NEAR
    info = info_ref[...].astype(jnp.bfloat16)
    for k in range(far):
        for j in range(NEAR):
            source = (k * NEAR + (near ^ j)) * depth
            if depth % 128 == 0:
                piece = x_ref[:, pl.ds(pl.multiple_of(source, 128), depth)]
            else:
                lane = source % 128
                wide = x_ref[:, pl.ds(pl.multiple_of(source - lane, 128), 128)]
                piece = wide[:, :depth]
                for first in range(depth, 128, depth):
                    piece = jnp.where(lane == first, wide[:, first:first + depth], piece)
            out_ref[k, :rows, j * depth:(j + 1) * depth] = piece
        out_ref[k, rows:, :rows] = info


def pack(x, info, me, far):
    rows, width = x.shape
    return pl.pallas_call(
        functools.partial(pack_kernel, far),
        out_shape=jax.ShapeDtypeStruct((far, rows + INFO, width // far), x.dtype),
        in_specs=[SMEM, VMEM, VMEM],
        out_specs=VMEM,
        compiler_params=params(16),
        cost_estimate=pl.CostEstimate(flops=0, bytes_accessed=4 * rows * width, transcendentals=0),
        name="pack",
    )(me, x, info)


def project_kernel(far, rows, *refs):
    w_refs, x_ref, out_ref = refs[:NEAR], refs[NEAR], refs[NEAR + 1]
    streams, depth, tile = w_refs[0].shape
    x = jnp.concatenate([x_ref[k, :rows] for k in range(far)], axis=0)
    ids = jnp.concatenate(
        [to_column(x_ref[k, rows:rows + 1, :rows].astype(jnp.float32)) for k in range(far)], axis=0
    )
    total = None
    for j in range(NEAR):
        part = x[:, j * depth:(j + 1) * depth]
        chosen = [jnp.where(ids == s, part, jnp.zeros_like(part)) for s in range(STREAMS)]
        term = jnp.dot(
            jnp.concatenate(chosen, axis=1),
            w_refs[j][...].reshape(streams * depth, tile),
            preferred_element_type=jnp.float32,
        )
        total = term if total is None else total + term
    for k in range(far):
        out_ref[k] = total[k * rows:(k + 1) * rows].astype(jnp.bfloat16)


def project(x_all, w_parts, offsets, columns):
    far, padded, width = x_all.shape
    rows = padded - INFO
    streams, depth, _ = w_parts[0].shape
    tile = min(256, columns)
    return pl.pallas_call(
        functools.partial(project_kernel, far, rows),
        grid=(columns // tile,),
        out_shape=jax.ShapeDtypeStruct((far, rows, columns), jnp.bfloat16),
        in_specs=[
            pl.BlockSpec((streams, depth, tile), lambda i, start=start // tile: (0, 0, i + start))
            for start in offsets
        ]
        + [pl.BlockSpec((far, padded, width), lambda i: (0, 0, 0))],
        out_specs=pl.BlockSpec((far, rows, tile), lambda i: (0, 0, i)),
        compiler_params=params(24),
        cost_estimate=pl.CostEstimate(
            flops=2 * far * rows * width * streams * columns,
            bytes_accessed=2 * (far * rows * (width + columns) + NEAR * streams * depth * columns),
            transcendentals=0,
        ),
        name="project",
    )(*w_parts, x_all)


def reduce_kernel(square_columns, *refs):
    half = len(refs) // 2
    squares = None
    for parts_ref, total_ref in zip(refs[:half], refs[half:-1]):
        total = parts_ref[0].astype(jnp.float32)
        for k in range(1, parts_ref.shape[0]):
            total = total + parts_ref[k].astype(jnp.float32)
        total_ref[...] = total
        for first in range(0, total.shape[1], 2 * HEAD_DIM):
            block = total[:, first:first + square_columns]
            term = jnp.sum(block * block, axis=1, keepdims=True)
            squares = term if squares is None else squares + term
    refs[-1][...] = to_row(squares)


def reduce(parts, square_columns):
    far, rows, columns = parts[0].shape
    return pl.pallas_call(
        functools.partial(reduce_kernel, square_columns),
        out_shape=[jax.ShapeDtypeStruct((rows, columns), jnp.float32)] * len(parts)
        + [jax.ShapeDtypeStruct((8, rows), jnp.float32)],
        in_specs=[VMEM] * len(parts),
        out_specs=[VMEM] * (len(parts) + 1),
        compiler_params=params(16),
        cost_estimate=pl.CostEstimate(
            flops=2 * len(parts) * far * rows * columns,
            bytes_accessed=3 * len(parts) * far * rows * columns,
            transcendentals=0,
        ),
        name="reduce",
    )(*parts)


def normalize_kernel(total_ref, square_ref, gain_ref, info_ref, out_ref):
    ids = to_column(info_ref[:1].astype(jnp.float32))
    scale = to_column(lax.rsqrt(square_ref[:1] / (KV_HEADS * HEAD_DIM) + epsilon))
    for g in range(gain_ref.shape[1] // HEAD_DIM):
        first = 2 * g * HEAD_DIM
        gain = by_stream(ids, gain_ref, g * HEAD_DIM, HEAD_DIM)
        key = total_ref[:, first:first + HEAD_DIM] * scale * gain
        out_ref[:, first:first + HEAD_DIM] = key.astype(jnp.bfloat16)
        value = total_ref[:, first + HEAD_DIM:first + 2 * HEAD_DIM]
        out_ref[:, first + HEAD_DIM:first + 2 * HEAD_DIM] = value.astype(jnp.bfloat16)


def normalize(total, squares, gain, info):
    return pl.pallas_call(
        normalize_kernel,
        out_shape=jax.ShapeDtypeStruct(total.shape, jnp.bfloat16),
        in_specs=[VMEM] * 4,
        out_specs=VMEM,
        compiler_params=params(16),
        cost_estimate=pl.CostEstimate(
            flops=4 * total.size, bytes_accessed=6 * total.size, transcendentals=0
        ),
        name="normalize",
    )(total, squares, gain, info)


def attend_kernel(kv_local, per_group, q_count, far, me_ref, map_ref, info_ref, square_ref, gain_ref,
                  *refs):
    q_refs, kv_refs = refs[:q_count], refs[q_count:q_count + NEAR]
    out_ref, score_ref = refs[-2:]
    rows, columns = q_refs[0].shape
    keys = far * rows
    kv_columns = kv_refs[0].shape[1]
    exponent = math.log2(math.e) / math.sqrt(HEAD_DIM)
    near = me_ref[0] % NEAR
    first_half = lax.broadcasted_iota(jnp.int32, (1, rows), 1) < rows // 2
    ids = to_column(info_ref[:1].astype(jnp.float32))
    q_scale = to_column(lax.rsqrt(square_ref[:1] / (HEADS * HEAD_DIM) + epsilon))

    key_times = []
    for j in range(NEAR):
        pieces = []
        for k in range(far):
            owner = k * NEAR + (near ^ j)
            row, lane = divmod(k * rows, kv_columns)
            local = kv_refs[j][keys + row:keys + row + 1, lane:lane + rows].astype(jnp.float32)
            block = jnp.where(first_half, map_ref[2 * owner], map_ref[2 * owner + 1])
            pieces.append((block * FRAMES).astype(jnp.float32) + local)
        key_times.append(jnp.concatenate(pieces, axis=1))
    local = info_ref[1:2].astype(jnp.float32)
    block = jnp.where(first_half, map_ref[2 * me_ref[0]], map_ref[2 * me_ref[0] + 1])
    query_times = to_column((block * FRAMES).astype(jnp.float32) + local)

    query_times = jnp.concatenate([query_times] * per_group, axis=0)
    for g in range(kv_local):
        queries = []
        for h in range(per_group):
            head = g * per_group + h
            chunk, first = divmod(head * HEAD_DIM, columns)
            gain = by_stream(ids, gain_ref, head * HEAD_DIM, HEAD_DIM)
            queries.append(q_refs[chunk][:, first:first + HEAD_DIM] * q_scale * gain)
        q = jnp.concatenate(queries, axis=0).astype(jnp.bfloat16)
        peak = None
        for j in range(NEAR):
            key = kv_refs[j][:keys, 2 * g * HEAD_DIM:(2 * g + 1) * HEAD_DIM]
            score = lax.dot_general(
                q, key, (((1,), (1,)), ((), ())), preferred_element_type=jnp.float32
            )
            score = jnp.where(key_times[j] <= query_times, score, -1e30)
            score_ref[j] = score
            top = jnp.max(score, axis=1, keepdims=True)
            peak = top if peak is None else jnp.maximum(peak, top)
        total = jnp.zeros((per_group * rows, 1), jnp.float32)
        mixed = jnp.zeros((per_group * rows, HEAD_DIM), jnp.float32)
        for j in range(NEAR):
            value = kv_refs[j][:keys, (2 * g + 1) * HEAD_DIM:(2 * g + 2) * HEAD_DIM]
            terms = jnp.exp2((score_ref[j] - peak) * exponent)
            total = total + jnp.sum(terms, axis=1, keepdims=True)
            mixed = mixed + jnp.dot(
                terms.astype(jnp.bfloat16), value, preferred_element_type=jnp.float32
            )
        out = (mixed / total).astype(out_ref.dtype)
        for h in range(per_group):
            first = (g * per_group + h) * HEAD_DIM
            out_ref[:, first:first + HEAD_DIM] = out[h * rows:(h + 1) * rows]


def attend(me, block_map, info, squares, q_gain, q_parts, kv_parts, far, kv_local, per_group):
    rows, columns = q_parts[0].shape
    keys = NEAR * far * rows
    count = rows * kv_local * per_group * keys
    return pl.pallas_call(
        functools.partial(attend_kernel, kv_local, per_group, len(q_parts), far),
        out_shape=jax.ShapeDtypeStruct((rows, columns * len(q_parts)), jnp.bfloat16),
        in_specs=[SMEM, SMEM] + [VMEM] * (3 + len(q_parts) + NEAR),
        out_specs=VMEM,
        scratch_shapes=[pltpu.VMEM((NEAR, per_group * rows, far * rows), jnp.float32)],
        compiler_params=params(40),
        cost_estimate=pl.CostEstimate(
            flops=4 * count * HEAD_DIM,
            bytes_accessed=4 * keys * kv_local * HEAD_DIM,
            transcendentals=count,
        ),
        name="attend",
    )(me, block_map, info, squares, q_gain, *q_parts, *kv_parts)


def body(activations, w_query, w_keyval, q_gain, k_gain, stream_ids, local_times, block_map):
    row_count = activations.shape[0]
    group_size = HEADS // KV_HEADS
    q_width = w_query.shape[2]
    q_local = q_width // HEAD_DIM
    per_group = min(group_size, q_local)
    kv_local = q_local // per_group
    replicas = max(1, lax.axis_size("head") // KV_HEADS)
    head_index = lax.axis_index("head")
    first_group = head_index * q_local // group_size
    size = lax.axis_size("seq")
    far = size // NEAR
    me = lax.axis_index("seq").reshape(1)

    info = jnp.pad(jnp.stack([stream_ids, local_times]), ((0, INFO - 2), (0, 0)))
    groups = [[f * NEAR + j for f in range(far)] for j in range(NEAR)]

    def exchange(parts):
        return lax.all_to_all(parts, "seq", 0, 0, axis_index_groups=groups)

    kv_width = kv_local * 2 * HEAD_DIM
    kv_weights = lax.dynamic_slice_in_dim(
        w_keyval, first_group * (2 * HEAD_DIM), kv_width, 2
    )
    q_chunks = 2 if q_width % 512 == 0 else 1
    chunk = q_width // q_chunks
    q_starts = range(0, q_width, chunk)
    q_weights = [w_query[:, :, start:start + chunk] for start in q_starts]

    packed = pack(activations, info, me, far)
    kv_other = swap(kv_weights, 2)
    q_others = [swap(after(q_weights[0], packed, kv_weights), 2)]
    x_all = exchange(packed)
    q_others += [swap(after(w, x_all, kv_other), 2) for w in q_weights[1:]]
    kv_core = swap(after(kv_weights, x_all), 1)
    q_core = swap(after(w_query, x_all), 1)

    def partial_sums(own, core, other, start, columns, gate):
        other_core = swap(after(other, gate), 1)
        return project(
            x_all, [own, core, other, other_core], [start, start, 0, 0], columns
        )

    gate = partial_sums(kv_weights, kv_core, kv_other, 0, kv_width, x_all)
    kv_total, key_sq = reduce([exchange(gate)], HEAD_DIM)
    key_sq = head_sum(jnp.where(head_index % replicas == 0, key_sq, jnp.float32(0.0)))
    kv_gain = lax.dynamic_slice_in_dim(k_gain, first_group * HEAD_DIM, kv_local * HEAD_DIM, 1)
    kv_rows = normalize(kv_total, key_sq, kv_gain, info)
    times = x_all[:, row_count + 1, :row_count].reshape(-1, kv_rows.shape[1])
    times = jnp.pad(times, ((0, -times.shape[0] % 16), (0, 0)))
    kv_here = exchange(jnp.broadcast_to(kv_rows, (far,) + kv_rows.shape))
    kv_here = jnp.concatenate([kv_here.reshape(far * row_count, -1), times])
    kv_other = swap(kv_here, 2)
    kv_parts = [kv_here, swap(kv_here, 1), kv_other, swap(kv_other, 1)]

    q_parts = []
    for other, start in zip(q_others, q_starts):
        gate = partial_sums(w_query, q_core, other, start, chunk, gate)
        q_parts.append(exchange(gate))
    *q_totals, query_sq = reduce(q_parts, 2 * HEAD_DIM)
    query_sq = head_sum(query_sq)
    return attend(
        me, block_map, info, query_sq, q_gain, q_totals, kv_parts, far, kv_local, per_group
    )


def solution(mesh):
    placed = (
        P("seq", None),
        P(None, "seq", "head"),
        P(None, "seq", None),
        P(None, "head"),
        P(),
        P("seq"),
        P("seq"),
        P(),
    )
    return jax.shard_map(
        body, mesh=mesh, in_specs=placed, out_specs=P("seq", "head"), check_vma=False
    )
```

time: 153 us -> 136 us (0.89)
  between operations: 13.3 us -> 0.17 us
  waiting for transfers between devices: 76.8 us -> 70.1 us
  Pallas kernels: 17.1 us -> 22.9 us
  local copies, waits for them, and re-layouts: 12.8 us -> 7.44 us
  other arithmetic: 0.03 us -> 2.68 us
    ppermute x18 -> x11, waiting for transfers between devices: 69.2 us -> 9.06 us  [swap(): return lax.ppermute(x, 'seq', [(i, i ^ mask) for i in range(size)])]
    all_to_all x0 -> x5, waiting for transfers between devices: none -> 56.7 us  [exchange(): return lax.all_to_all(parts, 'seq', 0, 0, axis_index_groups=groups)]
    all_to_all x0 -> x5, starting transfers between devices: none -> 22.4 us  [exchange(): return lax.all_to_all(parts, 'seq', 0, 0, axis_index_groups=groups)]
    ppermute x18 -> x11, starting transfers between devices: 27.7 us -> 6.87 us  [swap(): return lax.ppermute(x, 'seq', [(i, i ^ mask) for i in range(size)])]
    unnamed x39 -> x18, local copies, waits for them, and re-layouts: 10.5 us -> 3.62 us
    pallas_call x3, Pallas kernels: 0.48 us -> 3.67 us  [the longest x2 2.51 us: reduce(): pl.pallas_call(functools.partial(reduce_kernel, square_columns), out_shap...]
    all_gather x3 -> x0, waiting for transfers between devices: 3.18 us -> none  [near_weights(): lax.all_gather(w, 'seq', axis=1, tiled=True, axis_index_groups=groups)]
    pallas_call x3, Pallas kernels: 9.87 us -> 12.7 us  [project(): pl.pallas_call(functools.partial(project_kernel, far, rows), grid=(column...]
  transfers between devices with their start and end apart: 23 -> 18, of which waited for: 13 -> 9; matrix products, arithmetic and copies ran while one was open for 1% -> 4% of each run, Pallas kernels for 7% -> 11%
where the time goes in v2:
time: 136 us
  waiting for transfers between devices  70.1 us (52%)
  starting transfers between devices  32.3 us (24%)
  Pallas kernels  22.9 us (17%)
  local copies, waits for them, and re-layouts  7.44 us (5%)
  other arithmetic  2.68 us (2%)
    all_to_all x5, waiting for transfers between devices, exchange(): return lax.all_to_all(parts, 'seq', 0, 0, axis_index_groups=groups)  56.7 us
    all_to_all x5, starting transfers between devices, exchange(): return lax.all_to_all(parts, 'seq', 0, 0, axis_index_groups=groups)  22.4 us
    pallas_call x3, Pallas kernels, project(): pl.pallas_call(functools.partial(project_kernel, far, rows), grid=(column...  12.7 us
    ppermute x11, waiting for transfers between devices, swap(): return lax.ppermute(x, 'seq', [(i, i ^ mask) for i in range(size)])  9.06 us
    ppermute x11, starting transfers between devices, swap(): return lax.ppermute(x, 'seq', [(i, i ^ mask) for i in range(size)])  6.87 us
    pallas_call x1, Pallas kernels, attend(): pl.pallas_call(functools.partial(attend_kernel, kv_local, per_group, len(...  6.38 us
    ppermute x2, waiting for transfers between devices, head_sum(): x = x + lax.ppermute(x, 'head', [(i, i ^ step) for i in range(size)])  4.25 us
    unnamed x18, local copies, waits for them, and re-layouts  3.62 us
  transfers between devices with their start and end apart: 18, of which 9 were waited for; matrix products, arithmetic and copies ran while one was open for 4% of the time, Pallas kernels for 11%

profile of v2, /device:TPU:0, one launch (start us, length us, event | category | flops | bytes accessed | tf_op | source)
XLA Modules:
  0.0 135.5 jit_solution(4189012091515714913)
XLA Ops:
  3.2 6.3 %all-to-all-start = ((bf16[4,136,1024]{2,1,0:T(8,128)(2,1)}), bf16[4,136,1024]{2,1,0:T(8,128)(2,1)}, u32[]{:S(2)}, u32[]{:S(2)}) async-start(bf16[4,136,1024]{2,1,0:T(8,128)(2,1)} %pack.1), calls=%async_computation | async-start | bytes 2228224 | tf_op jit(solution)/shard_map/all_to_all | solution.py:300
  10.5 1.5 %collective-permute-start.3 = (bf16[3,256,512]{2,1,0:T(8,128)(2,1)}, bf16[3,256,512]{2,1,0:T(8,128)(2,1)}, u32[]{:S(2)}, u32[]{:S(2)}) collective-permute-start(bf16[3,256,512]{2,1,0:T(8,128)(2,1)} %constant_dynamic-slice_fusion.1.refs_0_), channel_id=1, source_target_pairs={{0,2},{1,3},{2,0},{3,1},{4,6},{5,7},{6,4},{7,5},{8,10},{9,11},{10,... | collective-permute-start | bytes 2359304 | tf_op jit(solution)/shard_map/ppermute | solution.py:32
  12.0 24.8 %all-to-all-done.refs_4_ = bf16[4,136,1024]{2,1,0:T(8,128)(2,1)} async-done(((bf16[4,136,1024]{2,1,0:T(8,128)(2,1)}), bf16[4,136,1024]{2,1,0:T(8,128)(2,1)}, u32[]{:S(2)}, u32[]{:S(2)}) %all-to-all-start) | async-done | bytes 1114144 | tf_op jit(solution)/shard_map/all_to_all | solution.py:300
  37.2 1.3 fusion.2
  38.5 1.5 %collective-permute-start.1 = (bf16[3,256,512]{2,1,0:T(8,128)(2,1)}, bf16[3,256,512]{2,1,0:T(8,128)(2,1)}, u32[]{:S(2)}, u32[]{:S(2)}) collective-permute-start(bf16[3,256,512]{2,1,0:T(8,128)(2,1)} %get-tuple-element.18), channel_id=1, source_target_pairs={{0,2},{1,3},{2,0},{3,1},{4,6},{5,7},{6,4},{7,5},{8,10},{9,11},{10,... | collective-permute-start | bytes 2359304 | tf_op jit(solution)/shard_map/ppermute | solution.py:32
  40.3 4.1 %project.3 = bf16[4,128,512]{2,1,0:T(8,128)(2,1)S(1)} custom-call(bf16[3,256,512]{2,1,0:T(8,128)(2,1)} %constant_dynamic-slice_fusion.1.refs_0_, bf16[3,256,512]{2,1,0:T(8,128)(2,1)S(1)} %collective-permute-done.2.refs_1_, bf16[3,256,512]{2,1,0:T(8,128)(2,1)} %collective-permute-done.3.refs_2_, bf16[3,256,512]{2,1,0:T(8,128)(2,1)S(1)} %collective-permute-done.4.refs_3_, ...), custom_call_target="tpu_custom_call" | custom-call | flops 1610612736 | bytes 4718592 | tf_op jit(solution)/shard_map/project/pallas_call | solution.py:122
  45.3 4.3 %all-to-all-start.3 = ((bf16[4,128,512]{2,1,0:T(8,128)(2,1)}), bf16[4,128,512]{2,1,0:T(8,128)(2,1)}, u32[]{:S(2)}, u32[]{:S(2)}) async-start(bf16[4,128,512]{2,1,0:T(8,128)(2,1)} %copy-done.5), calls=%async_computation.3 | async-start | bytes 1048576 | tf_op jit(solution)/shard_map/all_to_all | solution.py:300
  49.5 8.8 %collective-permute-done.1.refs_2_ = bf16[3,256,512]{2,1,0:T(8,128)(2,1)} collective-permute-done((bf16[3,256,512]{2,1,0:T(8,128)(2,1)}, bf16[3,256,512]{2,1,0:T(8,128)(2,1)}, u32[]{:S(2)}, u32[]{:S(2)}) %collective-permute-start.1) | collective-permute-done | bytes 786464 | tf_op jit(solution)/shard_map/ppermute | solution.py:32
  58.3 1.5 %collective-permute-start.6 = (bf16[3,256,512]{2,1,0:T(8,128)(2,1)}, bf16[3,256,512]{2,1,0:T(8,128)(2,1)}, u32[]{:S(2)}, u32[]{:S(2)}) collective-permute-start(bf16[3,256,512]{2,1,0:T(8,128)(2,1)} %get-tuple-element.22), channel_id=1, source_target_pairs={{0,2},{1,3},{2,0},{3,1},{4,6},{5,7},{6,4},{7,5},{8,10},{9,11},{10,... | collective-permute-start | bytes 2359304 | tf_op jit(solution)/shard_map/ppermute | solution.py:32
  59.8 5.0 %all-to-all-done.3.refs_0_ = bf16[4,128,512]{2,1,0:T(8,128)(2,1)} async-done(((bf16[4,128,512]{2,1,0:T(8,128)(2,1)}), bf16[4,128,512]{2,1,0:T(8,128)(2,1)}, u32[]{:S(2)}, u32[]{:S(2)}) %all-to-all-start.3) | async-done | bytes 524320 | tf_op jit(solution)/shard_map/all_to_all | solution.py:300
  66.0 1.5 %collective-permute-start.9 = (f32[8,128]{1,0:T(8,128)S(1)}, f32[8,128]{1,0:T(8,128)S(1)}, u32[]{:S(2)}, u32[]{:S(2)}) collective-permute-start(f32[8,128]{1,0:T(8,128)S(1)} %get-tuple-element.28), channel_id=1, source_target_pairs={{0,16},{16,0},{1,17},{17,1},{2,18},{18,2},{3,19},{19,3},{4,20},{20... | collective-permute-start | bytes 12296 | tf_op jit(solution)/shard_map/ppermute | solution.py:43
  67.5 2.1 %collective-permute-done.9 = f32[8,128]{1,0:T(8,128)S(1)} collective-permute-done((f32[8,128]{1,0:T(8,128)S(1)}, f32[8,128]{1,0:T(8,128)S(1)}, u32[]{:S(2)}, u32[]{:S(2)}) %collective-permute-start.9) | collective-permute-done | bytes 4128 | tf_op jit(solution)/shard_map/ppermute | solution.py:43
  70.7 4.1 %all-to-all-start.4 = ((bf16[4,128,512]{2,1,0:T(8,128)(2,1)}), bf16[4,128,512]{2,1,0:T(8,128)(2,1)}, u32[]{:S(2)}, u32[]{:S(2)}) async-start(bf16[4,128,512]{2,1,0:T(8,128)(2,1)} %broadcast_in_dim.5), calls=%async_computation.4 | async-start | bytes 1048576 | tf_op jit(solution)/shard_map/all_to_all | solution.py:300
  74.9 4.3 %project.4 = bf16[4,128,512]{2,1,0:T(8,128)(2,1)S(1)} custom-call(bf16[3,256,1024]{2,1,0:T(8,128)(2,1)S(1)} %copy-done.1, bf16[3,256,1024]{2,1,0:T(8,128)(2,1)} %collective-permute-done.refs_1_, bf16[3,256,512]{2,1,0:T(8,128)(2,1)} %collective-permute-done.1.refs_2_, bf16[3,256,512]{2,1,0:T(8,128)(2,1)} %collective-permute-done.5.refs_3_, ...), custom_call_target="tpu_custom_call" | custom-call | flops 1610612736 | bytes 4718592 | tf_op jit(solution)/shard_map/project/pallas_call | solution.py:122
  80.0 8.6 %all-to-all-done.4 = bf16[4,128,512]{2,1,0:T(8,128)(2,1)} async-done(((bf16[4,128,512]{2,1,0:T(8,128)(2,1)}), bf16[4,128,512]{2,1,0:T(8,128)(2,1)}, u32[]{:S(2)}, u32[]{:S(2)}) %all-to-all-start.4) | async-done | bytes 524320 | tf_op jit(solution)/shard_map/all_to_all | solution.py:300
  88.6 4.2 %all-to-all-start.1 = ((bf16[4,128,512]{2,1,0:T(8,128)(2,1)}), bf16[4,128,512]{2,1,0:T(8,128)(2,1)}, u32[]{:S(2)}, u32[]{:S(2)}) async-start(bf16[4,128,512]{2,1,0:T(8,128)(2,1)} %copy-done.2), calls=%async_computation.1 | async-start | bytes 1048576 | tf_op jit(solution)/shard_map/all_to_all | solution.py:300
  93.4 1.9 %fusion.1.refs_2_ = bf16[528,512]{1,0:T(8,128)(2,1)} fusion(bf16[1,512]{1,0:T(2,128)(2,1)S(1)} %slice_bitcast_fusion, bf16[512,512]{1,0:T(8,128)(2,1)} %bitcast.3), kind=kLoop, calls=%fused_computation.2 | loop fusion | flops 1622016 | bytes 1065984 | tf_op jit(solution)/shard_map/concatenate | solution.py:333
  96.6 4.3 %project.5 = bf16[4,128,512]{2,1,0:T(8,128)(2,1)S(1)} custom-call(bf16[3,256,1024]{2,1,0:T(8,128)(2,1)S(1)} %copy-done.1, bf16[3,256,1024]{2,1,0:T(8,128)(2,1)} %collective-permute-done.refs_1_, bf16[3,256,512]{2,1,0:T(8,128)(2,1)} %collective-permute-done.6.refs_2_, bf16[3,256,512]{2,1,0:T(8,128)(2,1)} %collective-permute-done.7.refs_3_, ...), custom_call_target="tpu_custom_call" | custom-call | flops 1610612736 | bytes 4718592 | tf_op jit(solution)/shard_map/project/pallas_call | solution.py:122
  101.7 5.1 %all-to-all-done.1.refs_0_ = bf16[4,128,512]{2,1,0:T(8,128)(2,1)} async-done(((bf16[4,128,512]{2,1,0:T(8,128)(2,1)}), bf16[4,128,512]{2,1,0:T(8,128)(2,1)}, u32[]{:S(2)}, u32[]{:S(2)}) %all-to-all-start.1) | async-done | bytes 524320 | tf_op jit(solution)/shard_map/all_to_all | solution.py:300
  106.7 3.5 %all-to-all-start.2 = ((bf16[4,128,512]{2,1,0:T(8,128)(2,1)}), bf16[4,128,512]{2,1,0:T(8,128)(2,1)S(1)}, u32[]{:S(2)}, u32[]{:S(2)}) async-start(bf16[4,128,512]{2,1,0:T(8,128)(2,1)} %copy-done.3), calls=%async_computation.2 | async-start | bytes 1048576 | tf_op jit(solution)/shard_map/all_to_all | solution.py:300
  110.8 13.4 %all-to-all-done.2.refs_1_ = bf16[4,128,512]{2,1,0:T(8,128)(2,1)S(1)} async-done(((bf16[4,128,512]{2,1,0:T(8,128)(2,1)}), bf16[4,128,512]{2,1,0:T(8,128)(2,1)S(1)}, u32[]{:S(2)}, u32[]{:S(2)}) %all-to-all-start.2) | async-done | bytes 524320 | tf_op jit(solution)/shard_map/all_to_all | solution.py:300
  125.5 1.5 %collective-permute-start.8 = (f32[8,128]{1,0:T(8,128)S(1)}, f32[8,128]{1,0:T(8,128)S(1)}, u32[]{:S(2)}, u32[]{:S(2)}) collective-permute-start(f32[8,128]{1,0:T(8,128)S(1)} %get-tuple-element.24), channel_id=1, source_target_pairs={{0,16},{16,0},{1,17},{17,1},{2,18},{18,2},{3,19},{19,3},{4,20},{20... | collective-permute-start | bytes 12296 | tf_op jit(solution)/shard_map/ppermute | solution.py:43
  127.0 2.1 %collective-permute-done.8 = f32[8,128]{1,0:T(8,128)S(1)} collective-permute-done((f32[8,128]{1,0:T(8,128)S(1)}, f32[8,128]{1,0:T(8,128)S(1)}, u32[]{:S(2)}, u32[]{:S(2)}) %collective-permute-start.8) | collective-permute-done | bytes 4128 | tf_op jit(solution)/shard_map/ppermute | solution.py:43
  129.1 6.4 %attend.1 = bf16[128,1024]{1,0:T(8,128)(2,1)} custom-call(s32[1]{0:T(128)} %bitcast.me_ref, s32[32]{0:T(128)S(1)} %copy-done.7, s32[8,128]{1,0:T(8,128)S(1)} %pad.8.info_ref, f32[8,128]{1,0:T(8,128)S(1)} %add.20.square_ref, f32[3,1024]{1,0:T(4,128)S(1)} %copy-done.6, f32[128,512]{1,0:T(8,128)S(1)} %get-tuple-element.25.refs_0_, ...), custom_call_target="tpu_custom_call" | custom-call | flops 1073741824 | bytes 2097152 | tf_op jit(solution)/shard_map/attend/pallas_call | solution.py:266
  (48 shorter events, 13.5 us)
Async XLA Ops:
  0.0 9.5 %copy-start = (bf16[3,256,1024]{2,1,0:T(8,128)(2,1)S(1)}, bf16[3,256,1024]{2,1,0:T(8,128)(2,1)}, u32[]{:S(2)}) copy-start(bf16[3,256,1024]{2,1,0:T(8,128)(2,1)} %param.10) | copy-start | bytes 4718596
  0.8 1.2 copy-start.4
  3.2 33.5 %all-to-all-start = ((bf16[4,136,1024]{2,1,0:T(8,128)(2,1)}), bf16[4,136,1024]{2,1,0:T(8,128)(2,1)}, u32[]{:S(2)}, u32[]{:S(2)}) async-start(bf16[4,136,1024]{2,1,0:T(8,128)(2,1)} %pack.1), calls=%async_computation | async-start | bytes 2228224 | tf_op jit(solution)/shard_map/all_to_all | solution.py:300
  9.5 27.7 %copy-start.1 = (bf16[3,256,1024]{2,1,0:T(8,128)(2,1)S(1)}, bf16[3,256,1024]{2,1,0:T(8,128)(2,1)}, u32[]{:S(2)}) copy-start(bf16[3,256,1024]{2,1,0:T(8,128)(2,1)} %refs_0_.3) | copy-start | bytes 4718596
  10.5 26.2 %collective-permute-start.3 = (bf16[3,256,512]{2,1,0:T(8,128)(2,1)}, bf16[3,256,512]{2,1,0:T(8,128)(2,1)}, u32[]{:S(2)}, u32[]{:S(2)}) collective-permute-start(bf16[3,256,512]{2,1,0:T(8,128)(2,1)} %constant_dynamic-slice_fusion.1.refs_0_), channel_id=1, source_target_pairs={{0,2},{1,3},{2,0},{3,1},{4,6},{5,7},{6,4},{7,5},{8,10},{9,11},{10,... | collective-permute-start | bytes 2359304 | tf_op jit(solution)/shard_map/ppermute | solution.py:32
  36.7 3.3 %collective-permute-start.2 = (bf16[3,256,512]{2,1,0:T(8,128)(2,1)}, bf16[3,256,512]{2,1,0:T(8,128)(2,1)S(1)}, u32[]{:S(2)}, u32[]{:S(2)}) collective-permute-start(bf16[3,256,512]{2,1,0:T(8,128)(2,1)} %constant_dynamic-slice_fusion.1.refs_0_), channel_id=1, source_target_pairs={{0,1},{1,0},{2,3},{3,2},{4,5},{5,4},{6,7},{7,6},{8,9},{9,8},{10,11... | collective-permute-start | bytes 2359304 | tf_op jit(solution)/shard_map/ppermute | solution.py:32
  36.7 3.6 %collective-permute-start.4 = (bf16[3,256,512]{2,1,0:T(8,128)(2,1)}, bf16[3,256,512]{2,1,0:T(8,128)(2,1)S(1)}, u32[]{:S(2)}, u32[]{:S(2)}) collective-permute-start(bf16[3,256,512]{2,1,0:T(8,128)(2,1)} %collective-permute-done.3.refs_2_), channel_id=1, source_target_pairs={{0,1},{1,0},{2,3},{3,2},{4,5},{5,4},{6,7},{7,6},{8,9},{9,8},{10,11... | collective-permute-start | bytes 2359304 | tf_op jit(solution)/shard_map/ppermute | solution.py:32
  38.5 19.8 %collective-permute-start.1 = (bf16[3,256,512]{2,1,0:T(8,128)(2,1)}, bf16[3,256,512]{2,1,0:T(8,128)(2,1)}, u32[]{:S(2)}, u32[]{:S(2)}) collective-permute-start(bf16[3,256,512]{2,1,0:T(8,128)(2,1)} %get-tuple-element.18), channel_id=1, source_target_pairs={{0,2},{1,3},{2,0},{3,1},{4,6},{5,7},{6,4},{7,5},{8,10},{9,11},{10,... | collective-permute-start | bytes 2359304 | tf_op jit(solution)/shard_map/ppermute | solution.py:32
  40.1 34.8 %collective-permute-start = (bf16[3,256,1024]{2,1,0:T(8,128)(2,1)S(1)}, bf16[3,256,1024]{2,1,0:T(8,128)(2,1)}, u32[]{:S(2)}, u32[]{:S(2)}) collective-permute-start(bf16[3,256,1024]{2,1,0:T(8,128)(2,1)S(1)} %copy-done.1), channel_id=1, source_target_pairs={{0,1},{1,0},{2,3},{3,2},{4,5},{5,4},{6,7},{7,6},{8,9},{9,8},{10,11... | collective-permute-start | bytes 4718600 | tf_op jit(solution)/shard_map/ppermute | solution.py:32
  45.3 22.3 %copy-start.8 = (f32[3,512]{1,0:T(4,128)S(1)}, f32[3,512]{1,0:T(4,128)}, u32[]{:S(2)}) copy-start(f32[3,512]{1,0:T(4,128)} %param.12) | copy-start | bytes 18436
  45.3 19.5 %all-to-all-start.3 = ((bf16[4,128,512]{2,1,0:T(8,128)(2,1)}), bf16[4,128,512]{2,1,0:T(8,128)(2,1)}, u32[]{:S(2)}, u32[]{:S(2)}) async-start(bf16[4,128,512]{2,1,0:T(8,128)(2,1)} %copy-done.5), calls=%async_computation.3 | async-start | bytes 1048576 | tf_op jit(solution)/shard_map/all_to_all | solution.py:300
  58.3 16.6 %collective-permute-start.5 = (bf16[3,256,512]{2,1,0:T(8,128)(2,1)}, bf16[3,256,512]{2,1,0:T(8,128)(2,1)}, u32[]{:S(2)}, u32[]{:S(2)}) collective-permute-start(bf16[3,256,512]{2,1,0:T(8,128)(2,1)} %collective-permute-done.1.refs_2_), channel_id=1, source_target_pairs={{0,1},{1,0},{2,3},{3,2},{4,5},{5,4},{6,7},{7,6},{8,9},{9,8},{10,11... | collective-permute-start | bytes 2359304 | tf_op jit(solution)/shard_map/ppermute | solution.py:32
  58.3 21.7 %collective-permute-start.6 = (bf16[3,256,512]{2,1,0:T(8,128)(2,1)}, bf16[3,256,512]{2,1,0:T(8,128)(2,1)}, u32[]{:S(2)}, u32[]{:S(2)}) collective-permute-start(bf16[3,256,512]{2,1,0:T(8,128)(2,1)} %get-tuple-element.22), channel_id=1, source_target_pairs={{0,2},{1,3},{2,0},{3,1},{4,6},{5,7},{6,4},{7,5},{8,10},{9,11},{10,... | collective-permute-start | bytes 2359304 | tf_op jit(solution)/shard_map/ppermute | solution.py:32
  66.0 3.6 %collective-permute-start.9 = (f32[8,128]{1,0:T(8,128)S(1)}, f32[8,128]{1,0:T(8,128)S(1)}, u32[]{:S(2)}, u32[]{:S(2)}) collective-permute-start(f32[8,128]{1,0:T(8,128)S(1)} %get-tuple-element.28), channel_id=1, source_target_pairs={{0,16},{16,0},{1,17},{17,1},{2,18},{18,2},{3,19},{19,3},{4,20},{20... | collective-permute-start | bytes 12296 | tf_op jit(solution)/shard_map/ppermute | solution.py:43
  70.7 17.8 %all-to-all-start.4 = ((bf16[4,128,512]{2,1,0:T(8,128)(2,1)}), bf16[4,128,512]{2,1,0:T(8,128)(2,1)}, u32[]{:S(2)}, u32[]{:S(2)}) async-start(bf16[4,128,512]{2,1,0:T(8,128)(2,1)} %broadcast_in_dim.5), calls=%async_computation.4 | async-start | bytes 1048576 | tf_op jit(solution)/shard_map/all_to_all | solution.py:300
  80.0 16.6 %collective-permute-start.7 = (bf16[3,256,512]{2,1,0:T(8,128)(2,1)}, bf16[3,256,512]{2,1,0:T(8,128)(2,1)}, u32[]{:S(2)}, u32[]{:S(2)}) collective-permute-start(bf16[3,256,512]{2,1,0:T(8,128)(2,1)} %collective-permute-done.6.refs_2_), channel_id=1, source_target_pairs={{0,1},{1,0},{2,3},{3,2},{4,5},{5,4},{6,7},{7,6},{8,9},{9,8},{10,11... | collective-permute-start | bytes 2359304 | tf_op jit(solution)/shard_map/ppermute | solution.py:32
  88.6 18.2 %all-to-all-start.1 = ((bf16[4,128,512]{2,1,0:T(8,128)(2,1)}), bf16[4,128,512]{2,1,0:T(8,128)(2,1)}, u32[]{:S(2)}, u32[]{:S(2)}) async-start(bf16[4,128,512]{2,1,0:T(8,128)(2,1)} %copy-done.2), calls=%async_computation.1 | async-start | bytes 1048576 | tf_op jit(solution)/shard_map/all_to_all | solution.py:300
  95.3 15.0 %collective-permute-start.11 = (bf16[528,512]{1,0:T(8,128)(2,1)}, bf16[528,512]{1,0:T(8,128)(2,1)}, u32[]{:S(2)}, u32[]{:S(2)}) collective-permute-start(bf16[528,512]{1,0:T(8,128)(2,1)} %fusion.1.refs_2_), channel_id=1, source_target_pairs={{0,2},{1,3},{2,0},{3,1},{4,6},{5,7},{6,4},{7,5},{8,10},{9,11},{10,... | collective-permute-start | bytes 1622024 | tf_op jit(solution)/shard_map/ppermute | solution.py:32
  101.7 27.5 %copy-start.6 = (f32[3,1024]{1,0:T(4,128)S(1)}, f32[3,1024]{1,0:T(4,128)}, u32[]{:S(2)}) copy-start(f32[3,1024]{1,0:T(4,128)} %gain_ref.1) | copy-start | bytes 36868
  101.7 27.5 %copy-start.7 = (s32[32]{0:T(128)S(1)}, s32[32]{0:T(128)}, u32[]{:S(2)}) copy-start(s32[32]{0:T(128)} %map_ref.1) | copy-start | bytes 388
  106.7 17.4 %all-to-all-start.2 = ((bf16[4,128,512]{2,1,0:T(8,128)(2,1)}), bf16[4,128,512]{2,1,0:T(8,128)(2,1)S(1)}, u32[]{:S(2)}, u32[]{:S(2)}) async-start(bf16[4,128,512]{2,1,0:T(8,128)(2,1)} %copy-done.3), calls=%async_computation.2 | async-start | bytes 1048576 | tf_op jit(solution)/shard_map/all_to_all | solution.py:300
  110.2 18.9 %collective-permute-start.10 = (bf16[528,512]{1,0:T(8,128)(2,1)}, bf16[528,512]{1,0:T(8,128)(2,1)S(1)}, u32[]{:S(2)}, u32[]{:S(2)}) collective-permute-start(bf16[528,512]{1,0:T(8,128)(2,1)} %fusion.1.refs_2_), channel_id=1, source_target_pairs={{0,1},{1,0},{2,3},{3,2},{4,5},{5,4},{6,7},{7,6},{8,9},{9,8},{10,11... | collective-permute-start | bytes 1622024 | tf_op jit(solution)/shard_map/ppermute | solution.py:32
  110.3 18.8 %collective-permute-start.12 = (bf16[528,512]{1,0:T(8,128)(2,1)}, bf16[528,512]{1,0:T(8,128)(2,1)}, u32[]{:S(2)}, u32[]{:S(2)}) collective-permute-start(bf16[528,512]{1,0:T(8,128)(2,1)} %collective-permute-done.11.refs_4_), channel_id=1, source_target_pairs={{0,1},{1,0},{2,3},{3,2},{4,5},{5,4},{6,7},{7,6},{8,9},{9,8},{10,11... | collective-permute-start | bytes 1622024 | tf_op jit(solution)/shard_map/ppermute | solution.py:32
  125.5 3.6 %collective-permute-start.8 = (f32[8,128]{1,0:T(8,128)S(1)}, f32[8,128]{1,0:T(8,128)S(1)}, u32[]{:S(2)}, u32[]{:S(2)}) collective-permute-start(f32[8,128]{1,0:T(8,128)S(1)} %get-tuple-element.24), channel_id=1, source_target_pairs={{0,16},{16,0},{1,17},{17,1},{2,18},{18,2},{3,19},{19,3},{4,20},{20... | collective-permute-start | bytes 12296 | tf_op jit(solution)/shard_map/ppermute | solution.py:43
  (3 other events, 2.4 us)

commit v3 on v2

v3 whole, which is shorter than its diff:
```python
import functools
import math

import jax
import jax.numpy as jnp
from jax import lax
from jax.experimental import pallas as pl
from jax.experimental.pallas import tpu as pltpu
from jax.sharding import PartitionSpec as P

HEADS = 16
KV_HEADS = 4
HEAD_DIM = 128
STREAMS = 3
FRAMES = 32
NEAR = 4
INFO = 8

epsilon = 1e-06
MIB = 1024 * 1024

VMEM = pl.BlockSpec(memory_space=pltpu.VMEM)
SMEM = pl.BlockSpec(memory_space=pltpu.SMEM)


def params(mib):
    return pltpu.CompilerParams(vmem_limit_bytes=mib * MIB)


def swap(x, mask):
    size = lax.axis_size("seq")
    return lax.ppermute(x, "seq", [(i, i ^ mask) for i in range(size)])


def head_swap(x):
    size = lax.axis_size("head")
    return lax.ppermute(x, "head", [(i, i ^ 1) for i in range(size)])


def after(x, *others):
    return lax.optimization_barrier((x,) + others)[0]


def head_sum(x):
    size = lax.axis_size("head")
    step = 1
    while step < size:
        x = x + lax.ppermute(x, "head", [(i, i ^ step) for i in range(size)])
        step *= 2
    return x


def to_row(column):
    return jnp.broadcast_to(column, (column.shape[0], 128)).T[:8]


def to_column(row):
    return jnp.broadcast_to(row, (128, row.shape[1])).T[:, :1]


def by_stream(ids, gain_ref, first, width):
    gain = jnp.zeros((ids.shape[0], width), jnp.float32)
    for s in range(STREAMS):
        gain = jnp.where(ids == s, gain_ref[s:s + 1, first:first + width], gain)
    return gain


def pack_kernel(far, me_ref, x_ref, info_ref, *out_refs):
    rows = x_ref.shape[0]
    depth = x_ref.shape[1] // (far * NEAR)
    me = me_ref[0]
    half = me_ref[1] * (NEAR // 2)
    info = info_ref[...].astype(jnp.bfloat16)
    for k in range(far):
        for j in range(NEAR if k == 0 else NEAR // 2):
            source = (me ^ (k * NEAR + (j if k == 0 else j + half))) * depth
            if depth % 128 == 0:
                piece = x_ref[:, pl.ds(pl.multiple_of(source, 128), depth)]
            else:
                lane = source % 128
                wide = x_ref[:, pl.ds(pl.multiple_of(source - lane, 128), 128)]
                piece = wide[:, :depth]
                for first in range(depth, 128, depth):
                    piece = jnp.where(lane == first, wide[:, first:first + depth], piece)
            out_refs[k][:rows, j * depth:(j + 1) * depth] = piece
        out_refs[k][rows:, :rows] = info


def pack(x, info, me, far):
    rows, width = x.shape
    width = width // far
    return pl.pallas_call(
        functools.partial(pack_kernel, far),
        out_shape=[jax.ShapeDtypeStruct((rows + INFO, width), x.dtype)]
        + [jax.ShapeDtypeStruct((rows + INFO, width // 2), x.dtype)] * (far - 1),
        in_specs=[SMEM, VMEM, VMEM],
        out_specs=[VMEM] * far,
        compiler_params=params(16),
        cost_estimate=pl.CostEstimate(flops=0, bytes_accessed=2 * x.size, transcendentals=0),
        name="pack",
    )(me, x, info)


def project_kernel(far, rows, me_ref, *refs):
    w_refs, x_refs = refs[:NEAR], refs[NEAR:NEAR + 2 * far - 1]
    out_refs, spread_ref = refs[NEAR + 2 * far - 1:-1], refs[-1]
    streams, depth, tile = w_refs[0].shape

    @pl.when(pl.program_id(0) == 0)
    def _():
        upper = me_ref[1] == 1
        for k in range(far):
            mine = x_refs[max(2 * k - 1, 0)]
            ids = to_column(mine[rows:rows + 1, :rows].astype(jnp.float32))
            for j in range(NEAR):
                if k == 0:
                    part = mine[:rows, j * depth:(j + 1) * depth]
                else:
                    first = j % (NEAR // 2) * depth
                    part = mine[:rows, first:first + depth]
                    theirs = x_refs[2 * k][:rows, first:first + depth]
                    part = jnp.where(upper == (j >= NEAR // 2), part, theirs)
                for s in range(streams):
                    first = (j * streams + s) * depth
                    spread_ref[k * rows:(k + 1) * rows, first:first + depth] = jnp.where(
                        ids == s, part, jnp.zeros_like(part)
                    )

    total = None
    for j in range(NEAR):
        term = jnp.dot(
            spread_ref[:, j * streams * depth:(j + 1) * streams * depth],
            w_refs[j][...].reshape(streams * depth, tile),
            preferred_element_type=jnp.float32,
        )
        total = term if total is None else total + term
    out_refs[0][...] = total[:rows]
    for k in range(1, far):
        out_refs[k][...] = total[k * rows:(k + 1) * rows].astype(jnp.bfloat16)


def project(me, x_parts, w_parts, offsets, columns):
    far = (len(x_parts) + 1) // 2
    padded, width = x_parts[0].shape
    rows = padded - INFO
    streams, depth, _ = w_parts[0].shape
    tile = min(256, columns)
    shapes = [jax.ShapeDtypeStruct((rows, columns), jnp.float32)]
    shapes += [jax.ShapeDtypeStruct((rows, columns), jnp.bfloat16)] * (far - 1)
    return pl.pallas_call(
        functools.partial(project_kernel, far, rows),
        grid=(columns // tile,),
        out_shape=shapes,
        in_specs=[SMEM]
        + [
            pl.BlockSpec((streams, depth, tile), lambda i, start=start // tile: (0, 0, i + start))
            for start in offsets
        ]
        + [pl.BlockSpec(part.shape, lambda i: (0, 0)) for part in x_parts],
        out_specs=[pl.BlockSpec((rows, tile), lambda i: (0, i))] * far,
        scratch_shapes=[pltpu.VMEM((far * rows, streams * width), jnp.bfloat16)],
        compiler_params=params(24),
        cost_estimate=pl.CostEstimate(
            flops=2 * far * rows * width * streams * columns,
            bytes_accessed=2 * (far * rows * (width + columns) + NEAR * streams * depth * columns),
            transcendentals=0,
        ),
        name="project",
    )(me, *w_parts, *x_parts)


def reduce_kernel(far, square_columns, *refs):
    part_refs, total_ref, square_ref = refs[:-2], refs[-2], refs[-1]
    squares = None
    start = 0
    for own_ref, *other_refs in (part_refs[c:c + far] for c in range(0, len(part_refs), far)):
        total = own_ref[...]
        for ref in other_refs:
            total = total + ref[...].astype(jnp.float32)
        total_ref[:, start:start + total.shape[1]] = total
        start += total.shape[1]
        for first in range(0, total.shape[1], 2 * HEAD_DIM):
            block = total[:, first:first + square_columns]
            term = jnp.sum(block * block, axis=1, keepdims=True)
            squares = term if squares is None else squares + term
    square_ref[...] = to_row(squares)


def reduce(part_lists, square_columns):
    rows = part_lists[0][0].shape[0]
    columns = sum(parts[0].shape[1] for parts in part_lists)
    far = len(part_lists[0])
    parts = [part for parts in part_lists for part in parts]
    return pl.pallas_call(
        functools.partial(reduce_kernel, far, square_columns),
        out_shape=[
            jax.ShapeDtypeStruct((rows, columns), jnp.float32),
            jax.ShapeDtypeStruct((8, rows), jnp.float32),
        ],
        in_specs=[VMEM] * len(parts),
        out_specs=[VMEM] * 2,
        compiler_params=params(16),
        cost_estimate=pl.CostEstimate(
            flops=2 * far * rows * columns, bytes_accessed=3 * far * rows * columns,
            transcendentals=0,
        ),
        name="reduce",
    )(*parts)


def normalize_kernel(total_ref, square_ref, gain_ref, x_ref, out_ref):
    rows = total_ref.shape[0]
    ids = to_column(x_ref[rows:rows + 1, :rows].astype(jnp.float32))
    scale = to_column(lax.rsqrt(square_ref[:1] / (KV_HEADS * HEAD_DIM) + epsilon))
    for g in range(gain_ref.shape[1] // HEAD_DIM):
        first = 2 * g * HEAD_DIM
        gain = by_stream(ids, gain_ref, g * HEAD_DIM, HEAD_DIM)
        key = total_ref[:, first:first + HEAD_DIM] * scale * gain
        out_ref[:, first:first + HEAD_DIM] = key.astype(jnp.bfloat16)
        value = total_ref[:, first + HEAD_DIM:first + 2 * HEAD_DIM]
        out_ref[:, first + HEAD_DIM:first + 2 * HEAD_DIM] = value.astype(jnp.bfloat16)


def normalize(total, squares, gain, x_own):
    return pl.pallas_call(
        normalize_kernel,
        out_shape=jax.ShapeDtypeStruct(total.shape, jnp.bfloat16),
        in_specs=[VMEM] * 4,
        out_specs=VMEM,
        compiler_params=params(16),
        cost_estimate=pl.CostEstimate(
            flops=4 * total.size, bytes_accessed=6 * total.size, transcendentals=0
        ),
        name="normalize",
    )(total, squares, gain, x_own)


def attend_kernel(kv_local, per_group, far, me_ref, map_ref, x_ref, square_ref, gain_ref, q_ref,
                  *refs):
    kv_refs, out_ref, score_ref = refs[:NEAR], refs[-2], refs[-1]
    rows = q_ref.shape[0]
    keys = far * rows
    kv_columns = kv_refs[0].shape[1]
    exponent = math.log2(math.e) / math.sqrt(HEAD_DIM)
    me = me_ref[0]
    first_half = lax.broadcasted_iota(jnp.int32, (1, rows), 1) < rows // 2
    ids = to_column(x_ref[rows:rows + 1, :rows].astype(jnp.float32))
    q_scale = to_column(lax.rsqrt(square_ref[:1] / (HEADS * HEAD_DIM) + epsilon))

    key_times = []
    for j in range(NEAR):
        pieces = []
        for k in range(far):
            owner = me ^ (k * NEAR + j)
            row, lane = divmod(k * rows, kv_columns)
            local = kv_refs[j][keys + row:keys + row + 1, lane:lane + rows].astype(jnp.float32)
            block = jnp.where(first_half, map_ref[2 * owner], map_ref[2 * owner + 1])
            pieces.append((block * FRAMES).astype(jnp.float32) + local)
        key_times.append(jnp.concatenate(pieces, axis=1))
    query_times = to_column(key_times[0][:, :rows])

    query_times = jnp.concatenate([query_times] * per_group, axis=0)
    for g in range(kv_local):
        queries = []
        for h in range(per_group):
            first = (g * per_group + h) * HEAD_DIM
            gain = by_stream(ids, gain_ref, first, HEAD_DIM)
            queries.append(q_ref[:, first:first + HEAD_DIM] * q_scale * gain)
        q = jnp.concatenate(queries, axis=0).astype(jnp.bfloat16)
        peak = None
        for j in range(NEAR):
            key = kv_refs[j][:keys, 2 * g * HEAD_DIM:(2 * g + 1) * HEAD_DIM]
            score = lax.dot_general(
                q, key, (((1,), (1,)), ((), ())), preferred_element_type=jnp.float32
            )
            score = jnp.where(key_times[j] <= query_times, score, -1e30)
            score_ref[j] = score
            top = jnp.max(score, axis=1, keepdims=True)
            peak = top if peak is None else jnp.maximum(peak, top)
        total = jnp.zeros((per_group * rows, 1), jnp.float32)
        mixed = jnp.zeros((per_group * rows, HEAD_DIM), jnp.float32)
        for j in range(NEAR):
            value = kv_refs[j][:keys, (2 * g + 1) * HEAD_DIM:(2 * g + 2) * HEAD_DIM]
            terms = jnp.exp2((score_ref[j] - peak) * exponent)
            total = total + jnp.sum(terms, axis=1, keepdims=True)
            mixed = mixed + jnp.dot(
                terms.astype(jnp.bfloat16), value, preferred_element_type=jnp.float32
            )
        out = (mixed / total).astype(out_ref.dtype)
        for h in range(per_group):
            first = (g * per_group + h) * HEAD_DIM
            out_ref[:, first:first + HEAD_DIM] = out[h * rows:(h + 1) * rows]


def attend(me, block_map, x_own, squares, q_gain, q, kv_parts, far, kv_local, per_group):
    rows = q.shape[0]
    keys = NEAR * far * rows
    count = rows * kv_local * per_group * keys
    return pl.pallas_call(
        functools.partial(attend_kernel, kv_local, per_group, far),
        out_shape=jax.ShapeDtypeStruct(q.shape, jnp.bfloat16),
        in_specs=[SMEM, SMEM] + [VMEM] * (4 + NEAR),
        out_specs=VMEM,
        scratch_shapes=[pltpu.VMEM((NEAR, per_group * rows, far * rows), jnp.float32)],
        compiler_params=params(40),
        cost_estimate=pl.CostEstimate(
            flops=4 * count * HEAD_DIM,
            bytes_accessed=4 * keys * kv_local * HEAD_DIM,
            transcendentals=count,
        ),
        name="attend",
    )(me, block_map, x_own, squares, q_gain, q, *kv_parts)


def body(activations, w_query, w_keyval, q_gain, k_gain, stream_ids, local_times, block_map):
    row_count = activations.shape[0]
    group_size = HEADS // KV_HEADS
    q_width = w_query.shape[2]
    q_local = q_width // HEAD_DIM
    per_group = min(group_size, q_local)
    kv_local = q_local // per_group
    replicas = max(1, lax.axis_size("head") // KV_HEADS)
    head_index = lax.axis_index("head")
    first_group = head_index * q_local // group_size
    size = lax.axis_size("seq")
    far = size // NEAR
    me = jnp.stack([lax.axis_index("seq"), head_index % 2])

    info = jnp.pad(jnp.stack([stream_ids, local_times]), ((0, INFO - 2), (0, 0)))
    packed = pack(activations, info, me, far)
    halves = [swap(packed[k], k * NEAR) for k in range(1, far)]
    x_parts = [packed[0]]
    for half in halves:
        x_parts += [half, head_swap(half)]

    kv_width = kv_local * 2 * HEAD_DIM
    kv_weights = lax.dynamic_slice_in_dim(
        w_keyval, first_group * (2 * HEAD_DIM), kv_width, 2
    )
    tiles = max(1, q_width // 256)
    q_widths = [width * q_width // tiles for width in (tiles - tiles // 2, tiles // 2) if width]
    q_starts = [sum(q_widths[:c]) for c in range(len(q_widths))]
    q_weights = [
        w_query[:, :, start:start + width] for start, width in zip(q_starts, q_widths)
    ]
    kv_other = swap(kv_weights, 2)
    q_others = [swap(q_weights[0], 2)]
    q_others += [swap(after(w, q_others[0]), 2) for w in q_weights[1:]]
    kv_core = swap(after(kv_weights, *x_parts), 1)

    def partial_sums(own, core, other, start, gate):
        other_core = swap(after(other, *gate), 1)
        parts = project(
            me, x_parts, [own, core, other, other_core], [start, start, 0, 0], other.shape[2]
        )
        return [parts[0]] + [swap(parts[k], k * NEAR) for k in range(1, far)], parts

    kv_parts, gate = partial_sums(kv_weights, kv_core, kv_other, 0, x_parts)
    q_core = swap(after(w_query, *gate), 1)
    kv_total, key_sq = reduce([kv_parts], HEAD_DIM)
    key_sq = head_sum(jnp.where(head_index % replicas == 0, key_sq, jnp.float32(0.0)))
    kv_gain = lax.dynamic_slice_in_dim(k_gain, first_group * HEAD_DIM, kv_local * HEAD_DIM, 1)
    kv_rows = normalize(kv_total, key_sq, kv_gain, x_parts[0])
    times = jnp.stack([part[row_count + 1, :row_count] for part in [packed[0]] + halves])
    times = times.reshape(-1, kv_rows.shape[1])
    times = jnp.pad(times, ((0, -times.shape[0] % 16), (0, 0)))
    kv_here = jnp.concatenate(
        [kv_rows] + [swap(kv_rows, k * NEAR) for k in range(1, far)] + [times]
    )
    q_parts, gate = [], [kv_total]
    for other, start in zip(q_others, q_starts):
        parts, sent = partial_sums(w_query, q_core, other, start, gate)
        q_parts.append(parts)
        if start == 0:
            kv_here = after(kv_here, *sent)
            kv_other = swap(kv_here, 2)
            gate = [kv_here]
            kv_core = swap(after(kv_here, *parts), 1)
            kv_parts = [kv_here, kv_core, kv_other, swap(after(kv_other, *parts), 1)]

    queries, query_sq = reduce(q_parts, 2 * HEAD_DIM)
    query_sq = head_sum(query_sq)
    return attend(
        me, block_map, x_parts[0], query_sq, q_gain, queries, kv_parts, far, kv_local, per_group
    )


def solution(mesh):
    placed = (
        P("seq", None),
        P(None, "seq", "head"),
        P(None, "seq", None),
        P(None, "head"),
        P(),
        P("seq"),
        P("seq"),
        P(),
    )
    return jax.shard_map(
        body, mesh=mesh, in_specs=placed, out_specs=P("seq", "head"), check_vma=False
    )
```

time: 136 us -> 125 us (0.919)
  waiting for transfers between devices: 70.1 us -> 58.5 us
  starting transfers between devices: 32.3 us -> 36.6 us
  Pallas kernels: 22.9 us -> 19.6 us
  other arithmetic: 2.68 us -> 0.1 us
  local copies, waits for them, and re-layouts: 7.44 us -> 9.42 us
    all_to_all x5 -> x0, waiting for transfers between devices: 56.7 us -> none  [exchange(): return lax.all_to_all(parts, 'seq', 0, 0, axis_index_groups=groups)]
    ppermute x11 -> x26, waiting for transfers between devices: 9.06 us -> 50.9 us  [swap(): return lax.ppermute(x, 'seq', [(i, i ^ mask) for i in range(size)])]
    ppermute x11 -> x26, starting transfers between devices: 6.87 us -> 31 us  [swap(): return lax.ppermute(x, 'seq', [(i, i ^ mask) for i in range(size)])]
    all_to_all x5 -> x0, starting transfers between devices: 22.4 us -> none  [exchange(): return lax.all_to_all(parts, 'seq', 0, 0, axis_index_groups=groups)]
    ppermute x0 -> x3, waiting for transfers between devices: none -> 4.52 us  [head_swap(): return lax.ppermute(x, 'head', [(i, i ^ 1) for i in range(size)])]
    ppermute x0 -> x3, starting transfers between devices: none -> 3.52 us  [head_swap(): return lax.ppermute(x, 'head', [(i, i ^ 1) for i in range(size)])]
    pallas_call x4, Pallas kernels: 10 us -> 7.66 us  [the longest x1 5.58 us: attend(): pl.pallas_call(functools.partial(attend_kernel, kv_local, per_group, far)...]
    slice x1 -> x5, local copies, waits for them, and re-layouts: 1.31 us -> 3.37 us  [the longest x4 2.05 us: body(): part[row_count + 1, :row_count]]
  transfers between devices with their start and end apart: 18 -> 31, of which waited for: 9 -> 15; matrix products, arithmetic and copies ran while one was open for 4% -> 3% of each run, Pallas kernels for 11% -> 11%
where the time goes in v3:
time: 125 us
  waiting for transfers between devices  58.5 us (47%)
  starting transfers between devices  36.6 us (29%)
  Pallas kernels  19.6 us (16%)
  local copies, waits for them, and re-layouts  9.42 us (8%)
    ppermute x26, waiting for transfers between devices, swap(): return lax.ppermute(x, 'seq', [(i, i ^ mask) for i in range(size)])  50.9 us
    ppermute x26, starting transfers between devices, swap(): return lax.ppermute(x, 'seq', [(i, i ^ mask) for i in range(size)])  31 us
    pallas_call x3, Pallas kernels, project(): pl.pallas_call(functools.partial(project_kernel, far, rows), grid=(column...  11.8 us
    pallas_call x1, Pallas kernels, attend(): pl.pallas_call(functools.partial(attend_kernel, kv_local, per_group, far)...  5.58 us
    ppermute x3, waiting for transfers between devices, head_swap(): return lax.ppermute(x, 'head', [(i, i ^ 1) for i in range(size)])  4.52 us
    unnamed x51, local copies, waits for them, and re-layouts  4.38 us
    ppermute x3, starting transfers between devices, head_swap(): return lax.ppermute(x, 'head', [(i, i ^ 1) for i in range(size)])  3.52 us
    ppermute x2, waiting for transfers between devices, head_sum(): x = x + lax.ppermute(x, 'head', [(i, i ^ step) for i in range(size)])  3.11 us
  transfers between devices with their start and end apart: 31, of which 15 were waited for; matrix products, arithmetic and copies ran while one was open for 3% of the time, Pallas kernels for 11%

profile of v3, /device:TPU:0, one launch (start us, length us, event | category | flops | bytes accessed | tf_op | source)
XLA Modules:
  0.0 124.6 jit_solution(1743232571282582680)
XLA Ops:
  2.4 3.0 %collective-permute-start.7 = (bf16[3,256,512]{2,1,0:T(8,128)(2,1)}, bf16[3,256,512]{2,1,0:T(8,128)(2,1)}, u32[]{:S(2)}, u32[]{:S(2)}) collective-permute-start(bf16[3,256,512]{2,1,0:T(8,128)(2,1)} %constant_dynamic-slice_fusion.1.refs_0_), channel_id=1, source_target_pairs={{0,2},{1,3},{2,0},{3,1},{4,6},{5,7},{6,4},{7,5},{8,10},{9,11},{10,... | collective-permute-start | bytes 2359304 | tf_op jit(solution)/shard_map/ppermute | solution.py:32
  9.0 2.6 %collective-permute-start.2 = (bf16[136,512]{1,0:T(8,128)(2,1)S(1)}, bf16[136,512]{1,0:T(8,128)(2,1)S(1)}, u32[]{:S(2)}, u32[]{:S(2)}) collective-permute-start(bf16[136,512]{1,0:T(8,128)(2,1)S(1)} %get-tuple-element.36), channel_id=1, source_target_pairs={{0,8},{1,9},{2,10},{3,11},{4,12},{5,13},{6,14},{7,15},{8,0},{9,1},... | collective-permute-start | bytes 417800 | tf_op jit(solution)/shard_map/ppermute | solution.py:32
  11.8 2.4 %collective-permute-done.refs_5_ = bf16[136,512]{1,0:T(8,128)(2,1)S(1)} collective-permute-done((bf16[136,512]{1,0:T(8,128)(2,1)S(1)}, bf16[136,512]{1,0:T(8,128)(2,1)S(1)}, u32[]{:S(2)}, u32[]{:S(2)}) %collective-permute-start) | collective-permute-done | bytes 139296 | tf_op jit(solution)/shard_map/ppermute | solution.py:32
  15.7 6.6 %collective-permute-done.2.refs_7_ = bf16[136,512]{1,0:T(8,128)(2,1)S(1)} collective-permute-done((bf16[136,512]{1,0:T(8,128)(2,1)S(1)}, bf16[136,512]{1,0:T(8,128)(2,1)S(1)}, u32[]{:S(2)}, u32[]{:S(2)}) %collective-permute-start.2) | collective-permute-done | bytes 139296 | tf_op jit(solution)/shard_map/ppermute | solution.py:32
  24.3 3.0 %collective-permute-done.3.refs_8_ = bf16[136,512]{1,0:T(8,128)(2,1)S(1)} collective-permute-done((bf16[136,512]{1,0:T(8,128)(2,1)S(1)}, bf16[136,512]{1,0:T(8,128)(2,1)S(1)}, u32[]{:S(2)}, u32[]{:S(2)}) %collective-permute-start.3) | collective-permute-done | bytes 139296 | tf_op jit(solution)/shard_map/ppermute | solution.py:37
  32.5 4.4 %project.3 = (f32[128,512]{1,0:T(8,128)S(1)}, bf16[128,512]{1,0:T(8,128)(2,1)}, bf16[128,512]{1,0:T(8,128)(2,1)}, bf16[128,512]{1,0:T(8,128)(2,1)}) custom-call(s32[2]{0:T(128)S(1)} %pad_add_fusion.1.me_ref, bf16[3,256,512]{2,1,0:T(8,128)(2,1)} %constant_dynamic-slice_fusion.1.refs_0_, bf16[3,256,512]{2,1,0:T(8,128)(2,1)S(1)} %collective-permute-done.6.refs_1_, ...), custom_call_target="tpu_custom_call" | custom-call | flops 1610612736 | bytes 4718592 | tf_op jit(solution)/shard_map/project/pallas_call | solution.py:150
  38.7 1.9 %collective-permute-start.12 = (bf16[128,512]{1,0:T(8,128)(2,1)}, bf16[128,512]{1,0:T(8,128)(2,1)}, u32[]{:S(2)}, u32[]{:S(2)}) collective-permute-start(bf16[128,512]{1,0:T(8,128)(2,1)} %get-tuple-element.42), channel_id=1, source_target_pairs={{0,8},{1,9},{2,10},{3,11},{4,12},{5,13},{6,14},{7,15},{8,0},{9,1},... | collective-permute-start | bytes 393224 | tf_op jit(solution)/shard_map/ppermute | solution.py:32
  42.1 3.7 %collective-permute-done.11.refs_1_ = bf16[128,512]{1,0:T(8,128)(2,1)S(1)} collective-permute-done((bf16[128,512]{1,0:T(8,128)(2,1)}, bf16[128,512]{1,0:T(8,128)(2,1)S(1)}, u32[]{:S(2)}, u32[]{:S(2)}) %collective-permute-start.11) | collective-permute-done | bytes 131104 | tf_op jit(solution)/shard_map/ppermute | solution.py:32
  45.8 6.2 %collective-permute-done.12.refs_2_ = bf16[128,512]{1,0:T(8,128)(2,1)} collective-permute-done((bf16[128,512]{1,0:T(8,128)(2,1)}, bf16[128,512]{1,0:T(8,128)(2,1)}, u32[]{:S(2)}, u32[]{:S(2)}) %collective-permute-start.12) | collective-permute-done | bytes 131104 | tf_op jit(solution)/shard_map/ppermute | solution.py:32
  59.3 2.6 %collective-permute-start.20 = (bf16[128,512]{1,0:T(8,128)(2,1)S(1)}, bf16[128,512]{1,0:T(8,128)(2,1)S(1)}, u32[]{:S(2)}, u32[]{:S(2)}) collective-permute-start(bf16[128,512]{1,0:T(8,128)(2,1)S(1)} %normalize.1), channel_id=1, source_target_pairs={{0,4},{1,5},{2,6},{3,7},{4,0},{5,1},{6,2},{7,3},{8,12},{9,13},{10,... | collective-permute-start | bytes 393224 | tf_op jit(solution)/shard_map/ppermute | solution.py:32
  62.5 4.2 %collective-permute-done.20 = bf16[128,512]{1,0:T(8,128)(2,1)S(1)} collective-permute-done((bf16[128,512]{1,0:T(8,128)(2,1)S(1)}, bf16[128,512]{1,0:T(8,128)(2,1)S(1)}, u32[]{:S(2)}, u32[]{:S(2)}) %collective-permute-start.20) | collective-permute-done | bytes 131104 | tf_op jit(solution)/shard_map/ppermute | solution.py:32
  66.7 1.9 %collective-permute-start.22 = (bf16[128,512]{1,0:T(8,128)(2,1)S(1)}, bf16[128,512]{1,0:T(8,128)(2,1)S(1)}, u32[]{:S(2)}, u32[]{:S(2)}) collective-permute-start(bf16[128,512]{1,0:T(8,128)(2,1)S(1)} %normalize.1), channel_id=1, source_target_pairs={{0,12},{1,13},{2,14},{3,15},{4,8},{5,9},{6,10},{7,11},{8,4},{9,5},... | collective-permute-start | bytes 393224 | tf_op jit(solution)/shard_map/ppermute | solution.py:32
  68.6 5.6 %collective-permute-done.21 = bf16[128,512]{1,0:T(8,128)(2,1)S(1)} collective-permute-done((bf16[128,512]{1,0:T(8,128)(2,1)S(1)}, bf16[128,512]{1,0:T(8,128)(2,1)S(1)}, u32[]{:S(2)}, u32[]{:S(2)}) %collective-permute-start.21) | collective-permute-done | bytes 131104 | tf_op jit(solution)/shard_map/ppermute | solution.py:32
  74.4 3.8 %project.4 = (f32[128,512]{1,0:T(8,128)S(1)}, bf16[128,512]{1,0:T(8,128)(2,1)S(1)}, bf16[128,512]{1,0:T(8,128)(2,1)S(1)}, bf16[128,512]{1,0:T(8,128)(2,1)S(1)}) custom-call(s32[2]{0:T(128)S(1)} %copy-done.6, bf16[3,256,1024]{2,1,0:T(8,128)(2,1)S(1)} %copy-done.1, bf16[3,256,1024]{2,1,0:T(8,128)(2,1)} %collective-permute-done.9.refs_1_, ...), custom_call_target="tpu_custom_call" | custom-call | flops 1610612736 | bytes 4718592 | tf_op jit(solution)/shard_map/project/pallas_call | solution.py:150
  79.8 2.6 %collective-permute-start.15 = (bf16[128,512]{1,0:T(8,128)(2,1)S(1)}, bf16[128,512]{1,0:T(8,128)(2,1)S(1)}, u32[]{:S(2)}, u32[]{:S(2)}) collective-permute-start(bf16[128,512]{1,0:T(8,128)(2,1)S(1)} %get-tuple-element.48), channel_id=1, source_target_pairs={{0,4},{1,5},{2,6},{3,7},{4,0},{5,1},{6,2},{7,3},{8,12},{9,13},{10,... | collective-permute-start | bytes 393224 | tf_op jit(solution)/shard_map/ppermute | solution.py:32
  84.8 3.8 %collective-permute-done.15.refs_1_ = bf16[128,512]{1,0:T(8,128)(2,1)S(1)} collective-permute-done((bf16[128,512]{1,0:T(8,128)(2,1)S(1)}, bf16[128,512]{1,0:T(8,128)(2,1)S(1)}, u32[]{:S(2)}, u32[]{:S(2)}) %collective-permute-start.15) | collective-permute-done | bytes 131104 | tf_op jit(solution)/shard_map/ppermute | solution.py:32
  88.7 6.6 %collective-permute-done.16.refs_2_ = bf16[128,512]{1,0:T(8,128)(2,1)S(1)} collective-permute-done((bf16[128,512]{1,0:T(8,128)(2,1)S(1)}, bf16[128,512]{1,0:T(8,128)(2,1)S(1)}, u32[]{:S(2)}, u32[]{:S(2)}) %collective-permute-start.16) | collective-permute-done | bytes 131104 | tf_op jit(solution)/shard_map/ppermute | solution.py:32
  95.8 3.6 %project.5 = (f32[128,512]{1,0:T(8,128)S(1)}, bf16[128,512]{1,0:T(8,128)(2,1)S(1)}, bf16[128,512]{1,0:T(8,128)(2,1)S(1)}, bf16[128,512]{1,0:T(8,128)(2,1)S(1)}) custom-call(s32[2]{0:T(128)S(1)} %copy-done.6, bf16[3,256,1024]{2,1,0:T(8,128)(2,1)S(1)} %copy-done.1, bf16[3,256,1024]{2,1,0:T(8,128)(2,1)} %collective-permute-done.9.refs_1_, ...), custom_call_target="tpu_custom_call" | custom-call | flops 1610612736 | bytes 4718592 | tf_op jit(solution)/shard_map/project/pallas_call | solution.py:150
  99.5 2.7 %collective-permute-start.24 = (bf16[128,512]{1,0:T(8,128)(2,1)S(1)}, bf16[128,512]{1,0:T(8,128)(2,1)S(1)}, u32[]{:S(2)}, u32[]{:S(2)}) collective-permute-start(bf16[128,512]{1,0:T(8,128)(2,1)S(1)} %get-tuple-element.56), channel_id=1, source_target_pairs={{0,4},{1,5},{2,6},{3,7},{4,0},{5,1},{6,2},{7,3},{8,12},{9,13},{10,... | collective-permute-start | bytes 393224 | tf_op jit(solution)/shard_map/ppermute | solution.py:32
  102.8 1.9 %collective-permute-start.26 = (bf16[128,512]{1,0:T(8,128)(2,1)S(1)}, bf16[128,512]{1,0:T(8,128)(2,1)S(1)}, u32[]{:S(2)}, u32[]{:S(2)}) collective-permute-start(bf16[128,512]{1,0:T(8,128)(2,1)S(1)} %get-tuple-element.58), channel_id=1, source_target_pairs={{0,12},{1,13},{2,14},{3,15},{4,8},{5,9},{6,10},{7,11},{8,4},{9,5},... | collective-permute-start | bytes 393224 | tf_op jit(solution)/shard_map/ppermute | solution.py:32
  104.6 2.8 %collective-permute-done.24.refs_5_ = bf16[128,512]{1,0:T(8,128)(2,1)S(1)} collective-permute-done((bf16[128,512]{1,0:T(8,128)(2,1)S(1)}, bf16[128,512]{1,0:T(8,128)(2,1)S(1)}, u32[]{:S(2)}, u32[]{:S(2)}) %collective-permute-start.24) | collective-permute-done | bytes 131104 | tf_op jit(solution)/shard_map/ppermute | solution.py:32
  107.4 7.7 %collective-permute-done.25.refs_6_ = bf16[128,512]{1,0:T(8,128)(2,1)S(1)} collective-permute-done((bf16[128,512]{1,0:T(8,128)(2,1)S(1)}, bf16[128,512]{1,0:T(8,128)(2,1)S(1)}, u32[]{:S(2)}, u32[]{:S(2)}) %collective-permute-start.25) | collective-permute-done | bytes 131104 | tf_op jit(solution)/shard_map/ppermute | solution.py:32
  115.9 3.1 %collective-permute-done.27 = f32[8,128]{1,0:T(8,128)S(1)} collective-permute-done((f32[8,128]{1,0:T(8,128)S(1)}, f32[8,128]{1,0:T(8,128)S(1)}, u32[]{:S(2)}, u32[]{:S(2)}) %collective-permute-start.27) | collective-permute-done | bytes 4128 | tf_op jit(solution)/shard_map/ppermute | solution.py:48
  119.0 5.6 %attend.1 = bf16[128,1024]{1,0:T(8,128)(2,1)} custom-call(s32[2]{0:T(128)S(1)} %copy-done.6, s32[32]{0:T(128)S(1)} %copy-done.20, bf16[136,1024]{1,0:T(8,128)(2,1)S(1)} %get-tuple-element.34.refs_4_.x_ref, f32[8,128]{1,0:T(8,128)S(1)} %add.26.square_ref, f32[3,1024]{1,0:T(4,128)S(1)} %copy-done.19, f32[128,1024]{1,0:T(8,128)S(1)} %get-tuple-element.60.q_ref, ...), custom_call_target="tpu_custom_call" | custom-call | flops 1073741824 | bytes 2097152 | tf_op jit(solution)/shard_map/attend/pallas_call | solution.py:299
  (111 shorter events, 32.1 us)
Async XLA Ops:
  2.4 26.4 %collective-permute-start.7 = (bf16[3,256,512]{2,1,0:T(8,128)(2,1)}, bf16[3,256,512]{2,1,0:T(8,128)(2,1)}, u32[]{:S(2)}, u32[]{:S(2)}) collective-permute-start(bf16[3,256,512]{2,1,0:T(8,128)(2,1)} %constant_dynamic-slice_fusion.1.refs_0_), channel_id=1, source_target_pairs={{0,2},{1,3},{2,0},{3,1},{4,6},{5,7},{6,4},{7,5},{8,10},{9,11},{10,... | collective-permute-start | bytes 2359304 | tf_op jit(solution)/shard_map/ppermute | solution.py:32
  9.0 13.3 %collective-permute-start.2 = (bf16[136,512]{1,0:T(8,128)(2,1)S(1)}, bf16[136,512]{1,0:T(8,128)(2,1)S(1)}, u32[]{:S(2)}, u32[]{:S(2)}) collective-permute-start(bf16[136,512]{1,0:T(8,128)(2,1)S(1)} %get-tuple-element.36), channel_id=1, source_target_pairs={{0,8},{1,9},{2,10},{3,11},{4,12},{5,13},{6,14},{7,15},{8,0},{9,1},... | collective-permute-start | bytes 417800 | tf_op jit(solution)/shard_map/ppermute | solution.py:32
  11.6 12.2 %collective-permute-start.4 = (bf16[136,512]{1,0:T(8,128)(2,1)S(1)}, bf16[136,512]{1,0:T(8,128)(2,1)S(1)}, u32[]{:S(2)}, u32[]{:S(2)}) collective-permute-start(bf16[136,512]{1,0:T(8,128)(2,1)S(1)} %get-tuple-element.37), channel_id=1, source_target_pairs={{0,12},{1,13},{2,14},{3,15},{4,8},{5,9},{6,10},{7,11},{8,4},{9,5},... | collective-permute-start | bytes 417800 | tf_op jit(solution)/shard_map/ppermute | solution.py:32
  14.2 10.1 %collective-permute-start.1 = (bf16[136,512]{1,0:T(8,128)(2,1)S(1)}, bf16[136,512]{1,0:T(8,128)(2,1)S(1)}, u32[]{:S(2)}, u32[]{:S(2)}) collective-permute-start(bf16[136,512]{1,0:T(8,128)(2,1)S(1)} %collective-permute-done.refs_5_), channel_id=1, source_target_pairs={{0,16},{16,0},{1,17},{17,1},{2,18},{18,2},{3,19},{19,3},{4,20},{20... | collective-permute-start | bytes 417800 | tf_op jit(solution)/shard_map/ppermute | solution.py:37
  30.6 23.5 %collective-permute-start.10 = (bf16[3,256,512]{2,1,0:T(8,128)(2,1)}, bf16[3,256,512]{2,1,0:T(8,128)(2,1)}, u32[]{:S(2)}, u32[]{:S(2)}) collective-permute-start(bf16[3,256,512]{2,1,0:T(8,128)(2,1)} %get-tuple-element.64), channel_id=1, source_target_pairs={{0,2},{1,3},{2,0},{3,1},{4,6},{5,7},{6,4},{7,5},{8,10},{9,11},{10,... | collective-permute-start | bytes 2359304 | tf_op jit(solution)/shard_map/ppermute | solution.py:32
  37.6 36.7 %collective-permute-start.9 = (bf16[3,256,1024]{2,1,0:T(8,128)(2,1)S(1)}, bf16[3,256,1024]{2,1,0:T(8,128)(2,1)}, u32[]{:S(2)}, u32[]{:S(2)}) collective-permute-start(bf16[3,256,1024]{2,1,0:T(8,128)(2,1)S(1)} %copy-done.1), channel_id=1, source_target_pairs={{0,1},{1,0},{2,3},{3,2},{4,5},{5,4},{6,7},{7,6},{8,9},{9,8},{10,11... | collective-permute-start | bytes 4718600 | tf_op jit(solution)/shard_map/ppermute | solution.py:32
  37.7 8.1 %collective-permute-start.11 = (bf16[128,512]{1,0:T(8,128)(2,1)}, bf16[128,512]{1,0:T(8,128)(2,1)S(1)}, u32[]{:S(2)}, u32[]{:S(2)}) collective-permute-start(bf16[128,512]{1,0:T(8,128)(2,1)} %get-tuple-element.41), channel_id=1, source_target_pairs={{0,4},{1,5},{2,6},{3,7},{4,0},{5,1},{6,2},{7,3},{8,12},{9,13},{10,... | collective-permute-start | bytes 393224 | tf_op jit(solution)/shard_map/ppermute | solution.py:32
  38.7 13.2 %collective-permute-start.12 = (bf16[128,512]{1,0:T(8,128)(2,1)}, bf16[128,512]{1,0:T(8,128)(2,1)}, u32[]{:S(2)}, u32[]{:S(2)}) collective-permute-start(bf16[128,512]{1,0:T(8,128)(2,1)} %get-tuple-element.42), channel_id=1, source_target_pairs={{0,8},{1,9},{2,10},{3,11},{4,12},{5,13},{6,14},{7,15},{8,0},{9,1},... | collective-permute-start | bytes 393224 | tf_op jit(solution)/shard_map/ppermute | solution.py:32
  40.6 11.3 %collective-permute-start.13 = (bf16[128,512]{1,0:T(8,128)(2,1)}, bf16[128,512]{1,0:T(8,128)(2,1)}, u32[]{:S(2)}, u32[]{:S(2)}) collective-permute-start(bf16[128,512]{1,0:T(8,128)(2,1)} %get-tuple-element.43), channel_id=1, source_target_pairs={{0,12},{1,13},{2,14},{3,15},{4,8},{5,9},{6,10},{7,11},{8,4},{9,5},... | collective-permute-start | bytes 393224 | tf_op jit(solution)/shard_map/ppermute | solution.py:32
  54.2 20.1 %collective-permute-start.14 = (bf16[3,256,512]{2,1,0:T(8,128)(2,1)}, bf16[3,256,512]{2,1,0:T(8,128)(2,1)S(1)}, u32[]{:S(2)}, u32[]{:S(2)}) collective-permute-start(bf16[3,256,512]{2,1,0:T(8,128)(2,1)} %collective-permute-done.10.refs_2_), channel_id=1, source_target_pairs={{0,1},{1,0},{2,3},{3,2},{4,5},{5,4},{6,7},{7,6},{8,9},{9,8},{10,11... | collective-permute-start | bytes 2359304 | tf_op jit(solution)/shard_map/ppermute | solution.py:32
  58.5 21.2 %collective-permute-start.18 = (bf16[3,256,512]{2,1,0:T(8,128)(2,1)}, bf16[3,256,512]{2,1,0:T(8,128)(2,1)S(1)}, u32[]{:S(2)}, u32[]{:S(2)}) collective-permute-start(bf16[3,256,512]{2,1,0:T(8,128)(2,1)} %get-tuple-element.51), channel_id=1, source_target_pairs={{0,2},{1,3},{2,0},{3,1},{4,6},{5,7},{6,4},{7,5},{8,10},{9,11},{10,... | collective-permute-start | bytes 2359304 | tf_op jit(solution)/shard_map/ppermute | solution.py:32
  59.3 7.4 %collective-permute-start.20 = (bf16[128,512]{1,0:T(8,128)(2,1)S(1)}, bf16[128,512]{1,0:T(8,128)(2,1)S(1)}, u32[]{:S(2)}, u32[]{:S(2)}) collective-permute-start(bf16[128,512]{1,0:T(8,128)(2,1)S(1)} %normalize.1), channel_id=1, source_target_pairs={{0,4},{1,5},{2,6},{3,7},{4,0},{5,1},{6,2},{7,3},{8,12},{9,13},{10,... | collective-permute-start | bytes 393224 | tf_op jit(solution)/shard_map/ppermute | solution.py:32
  61.9 12.3 %collective-permute-start.21 = (bf16[128,512]{1,0:T(8,128)(2,1)S(1)}, bf16[128,512]{1,0:T(8,128)(2,1)S(1)}, u32[]{:S(2)}, u32[]{:S(2)}) collective-permute-start(bf16[128,512]{1,0:T(8,128)(2,1)S(1)} %normalize.1), channel_id=1, source_target_pairs={{0,8},{1,9},{2,10},{3,11},{4,12},{5,13},{6,14},{7,15},{8,0},{9,1},... | collective-permute-start | bytes 393224 | tf_op jit(solution)/shard_map/ppermute | solution.py:32
  66.7 7.6 %collective-permute-start.22 = (bf16[128,512]{1,0:T(8,128)(2,1)S(1)}, bf16[128,512]{1,0:T(8,128)(2,1)S(1)}, u32[]{:S(2)}, u32[]{:S(2)}) collective-permute-start(bf16[128,512]{1,0:T(8,128)(2,1)S(1)} %normalize.1), channel_id=1, source_target_pairs={{0,12},{1,13},{2,14},{3,15},{4,8},{5,9},{6,10},{7,11},{8,4},{9,5},... | collective-permute-start | bytes 393224 | tf_op jit(solution)/shard_map/ppermute | solution.py:32
  78.2 17.1 %collective-permute-start.29 = (bf16[528,512]{1,0:T(8,128)(2,1)S(1)}, bf16[528,512]{1,0:T(8,128)(2,1)S(1)}, u32[]{:S(2)}, u32[]{:S(2)}) collective-permute-start(bf16[528,512]{1,0:T(8,128)(2,1)S(1)} %pad_dynamic-update-slice_fusion.refs_0_), channel_id=1, source_target_pairs={{0,2},{1,3},{2,0},{3,1},{4,6},{5,7},{6,4},{7,5},{8,10},{9,11},{10,... | collective-permute-start | bytes 1622024 | tf_op jit(solution)/shard_map/ppermute | solution.py:32
  79.8 16.1 %collective-permute-start.23 = (bf16[3,256,512]{2,1,0:T(8,128)(2,1)S(1)}, bf16[3,256,512]{2,1,0:T(8,128)(2,1)S(1)}, u32[]{:S(2)}, u32[]{:S(2)}) collective-permute-start(bf16[3,256,512]{2,1,0:T(8,128)(2,1)S(1)} %collective-permute-done.18.refs_2_), channel_id=1, source_target_pairs={{0,1},{1,0},{2,3},{3,2},{4,5},{5,4},{6,7},{7,6},{8,9},{9,8},{10,11... | collective-permute-start | bytes 2359304 | tf_op jit(solution)/shard_map/ppermute | solution.py:32
  79.8 8.9 %collective-permute-start.15 = (bf16[128,512]{1,0:T(8,128)(2,1)S(1)}, bf16[128,512]{1,0:T(8,128)(2,1)S(1)}, u32[]{:S(2)}, u32[]{:S(2)}) collective-permute-start(bf16[128,512]{1,0:T(8,128)(2,1)S(1)} %get-tuple-element.48), channel_id=1, source_target_pairs={{0,4},{1,5},{2,6},{3,7},{4,0},{5,1},{6,2},{7,3},{8,12},{9,13},{10,... | collective-permute-start | bytes 393224 | tf_op jit(solution)/shard_map/ppermute | solution.py:32
  82.4 12.9 %collective-permute-start.16 = (bf16[128,512]{1,0:T(8,128)(2,1)S(1)}, bf16[128,512]{1,0:T(8,128)(2,1)S(1)}, u32[]{:S(2)}, u32[]{:S(2)}) collective-permute-start(bf16[128,512]{1,0:T(8,128)(2,1)S(1)} %get-tuple-element.49), channel_id=1, source_target_pairs={{0,8},{1,9},{2,10},{3,11},{4,12},{5,13},{6,14},{7,15},{8,0},{9,1},... | collective-permute-start | bytes 393224 | tf_op jit(solution)/shard_map/ppermute | solution.py:32
  83.0 12.3 %collective-permute-start.17 = (bf16[128,512]{1,0:T(8,128)(2,1)S(1)}, bf16[128,512]{1,0:T(8,128)(2,1)S(1)}, u32[]{:S(2)}, u32[]{:S(2)}) collective-permute-start(bf16[128,512]{1,0:T(8,128)(2,1)S(1)} %get-tuple-element.50), channel_id=1, source_target_pairs={{0,12},{1,13},{2,14},{3,15},{4,8},{5,9},{6,10},{7,11},{8,4},{9,5},... | collective-permute-start | bytes 393224 | tf_op jit(solution)/shard_map/ppermute | solution.py:32
  95.3 23.7 %collective-permute-start.28 = (bf16[528,512]{1,0:T(8,128)(2,1)S(1)}, bf16[528,512]{1,0:T(8,128)(2,1)S(1)}, u32[]{:S(2)}, u32[]{:S(2)}) collective-permute-start(bf16[528,512]{1,0:T(8,128)(2,1)S(1)} %pad_dynamic-update-slice_fusion.refs_0_), channel_id=1, source_target_pairs={{0,1},{1,0},{2,3},{3,2},{4,5},{5,4},{6,7},{7,6},{8,9},{9,8},{10,11... | collective-permute-start | bytes 1622024 | tf_op jit(solution)/shard_map/ppermute | solution.py:32
  95.3 23.7 %collective-permute-start.30 = (bf16[528,512]{1,0:T(8,128)(2,1)S(1)}, bf16[528,512]{1,0:T(8,128)(2,1)S(1)}, u32[]{:S(2)}, u32[]{:S(2)}) collective-permute-start(bf16[528,512]{1,0:T(8,128)(2,1)S(1)} %collective-permute-done.29.refs_2_), channel_id=1, source_target_pairs={{0,1},{1,0},{2,3},{3,2},{4,5},{5,4},{6,7},{7,6},{8,9},{9,8},{10,11... | collective-permute-start | bytes 1622024 | tf_op jit(solution)/shard_map/ppermute | solution.py:32
  99.5 8.0 %collective-permute-start.24 = (bf16[128,512]{1,0:T(8,128)(2,1)S(1)}, bf16[128,512]{1,0:T(8,128)(2,1)S(1)}, u32[]{:S(2)}, u32[]{:S(2)}) collective-permute-start(bf16[128,512]{1,0:T(8,128)(2,1)S(1)} %get-tuple-element.56), channel_id=1, source_target_pairs={{0,4},{1,5},{2,6},{3,7},{4,0},{5,1},{6,2},{7,3},{8,12},{9,13},{10,... | collective-permute-start | bytes 393224 | tf_op jit(solution)/shard_map/ppermute | solution.py:32
  102.2 12.9 %collective-permute-start.25 = (bf16[128,512]{1,0:T(8,128)(2,1)S(1)}, bf16[128,512]{1,0:T(8,128)(2,1)S(1)}, u32[]{:S(2)}, u32[]{:S(2)}) collective-permute-start(bf16[128,512]{1,0:T(8,128)(2,1)S(1)} %get-tuple-element.57), channel_id=1, source_target_pairs={{0,8},{1,9},{2,10},{3,11},{4,12},{5,13},{6,14},{7,15},{8,0},{9,1},... | collective-permute-start | bytes 393224 | tf_op jit(solution)/shard_map/ppermute | solution.py:32
  102.8 12.3 %collective-permute-start.26 = (bf16[128,512]{1,0:T(8,128)(2,1)S(1)}, bf16[128,512]{1,0:T(8,128)(2,1)S(1)}, u32[]{:S(2)}, u32[]{:S(2)}) collective-permute-start(bf16[128,512]{1,0:T(8,128)(2,1)S(1)} %get-tuple-element.58), channel_id=1, source_target_pairs={{0,12},{1,13},{2,14},{3,15},{4,8},{5,9},{6,10},{7,11},{8,4},{9,5},... | collective-permute-start | bytes 393224 | tf_op jit(solution)/shard_map/ppermute | solution.py:32
  (30 other events, 386.8 us)
